TPU v7x, 128 devices: a whole 4x4x4 slice. The times are simulated.
128 devices in a mesh: owner: 32 (over z, y, core), split: 4 (over x).
Axes of the slice: x: 4, y: 4, z: 4, core: 2. Of those that a mesh axis runs over, the one named last changes fastest.
Arguments:
- emb: bfloat16 [16384, 1024], P(('owner', 'split')), may hold values from -130 to 130
- cluster: int32 [16384], P(('owner', 'split')), may hold values from 0 to 63, as said below
- owner_of: int32 [64], replicated, may hold values from 0 to 31, as said below
Outputs:
- best_cosine: float32 [16384], P(('owner', 'split'))
Inputs may be any that keep to these rules, and one draw needn't show every extreme that they name: Every cluster holds at least two rows. Together with owner_of: the rows of one device whose cluster is placed on one owner number at most 8, and on every device exactly 8 for some owner. `owner_of`: each owner holds exactly 2 clusters.
All inputs are finite; a program needn't handle non-finite values.
Results may differ from a plain program's by a relative error of at most 0.00053.
Values may be sent and summed in bfloat16 or wider, within the bound.
A program may use at most 64 MiB of HBM per device.

v0:
```python
import jax
import jax.numpy as jnp
from jax import lax
from jax.sharding import PartitionSpec as P


def row_best(rows_a, labels_a, place_a, rows_b, labels_b, place_b):
    scores = lax.dot_general(
        rows_a, rows_b, (((1,), (1,)), ((), ())), preferred_element_type=jnp.float32
    )
    same = (
        (labels_a[:, None] == labels_b[None, :])
        & (labels_b[None, :] >= 0)
        & (place_a[:, None] != place_b[None, :])
    )
    return jnp.max(jnp.where(same, scores, jnp.float32(-2.0)), 1)


def on_device(emb, cluster, owner_of):
    owners = lax.axis_size("owner")
    splits = lax.axis_size("split")
    rows = emb.shape[0]
    width = emb.shape[1]
    capacity = 2 * rows // owners
    held = owners * capacity
    values = emb.astype(jnp.float32)
    unit = (values * lax.rsqrt(jnp.sum(values * values, 1, keepdims=True) + 1e-06)).astype(
        jnp.bfloat16
    )
    cluster_hit = cluster[:, None] == jnp.arange(owner_of.shape[0], dtype=jnp.int32)[None, :]
    row_owner = jnp.sum(jnp.where(cluster_hit, owner_of[None, :], 0), 1)
    owner_hot = (row_owner[:, None] == jnp.arange(owners, dtype=jnp.int32)[None, :]).astype(
        jnp.int32
    )
    rank = jnp.sum(jnp.cumsum(owner_hot, 0) * owner_hot, 1) - 1
    slot = row_owner * capacity + rank
    source = jnp.full((held,), -1, jnp.int32).at[slot].set(jnp.arange(rows, dtype=jnp.int32))
    valid = source >= 0
    picked = jnp.maximum(source, 0)
    send_rows = jnp.where(valid[:, None], unit[picked], jnp.zeros((), jnp.bfloat16)).reshape(
        owners, capacity, width
    )
    send_labels = jnp.where(valid, cluster[picked], -1).reshape(owners, capacity)
    my_split = lax.axis_index("split")
    wide_rows = jnp.broadcast_to(send_rows[:, None], (owners, splits, capacity, width)).reshape(
        owners * splits, capacity, width
    )
    wide_labels = jnp.broadcast_to(send_labels[:, None], (owners, splits, capacity)).reshape(
        owners * splits, capacity
    )
    got_rows, got_labels = (
        lax.all_to_all(wide_rows, ("owner", "split"), split_axis=0, concat_axis=0, tiled=True),
        lax.all_to_all(wide_labels, ("owner", "split"), split_axis=0, concat_axis=0, tiled=True),
    )
    group_rows = got_rows.reshape(owners, splits, capacity, width)
    group_labels = got_labels.reshape(owners, splits, capacity)
    own_rows = lax.dynamic_index_in_dim(group_rows, my_split, 1, keepdims=False).reshape(
        held, width
    )
    own_labels = lax.dynamic_index_in_dim(group_labels, my_split, 1, keepdims=False).reshape(held)
    sender = jnp.arange(owners, dtype=jnp.int32)[:, None]
    column = jnp.arange(capacity, dtype=jnp.int32)[None, :]
    own_place = ((sender * splits + my_split) * capacity + column).reshape(held)
    all_place = jnp.arange(owners * splits * capacity, dtype=jnp.int32)
    best = row_best(
        own_rows,
        own_labels,
        own_place,
        group_rows.reshape(owners * splits * capacity, width),
        group_labels.reshape(owners * splits * capacity),
        all_place,
    )
    returned = lax.all_to_all(
        best.reshape(owners, capacity), "owner", split_axis=0, concat_axis=0, tiled=True
    )
    return returned.reshape(held)[slot]


def solution(mesh):
    return jax.shard_map(
        on_device,
        mesh=mesh,
        in_specs=(P(("owner", "split"), None), P(("owner", "split")), P()),
        out_specs=P(("owner", "split")),
        check_vma=False,
    )
```

profile of v0, /device:TPU:1, one launch (start us, length us, event | category | flops | bytes accessed | tf_op | source)
XLA Modules:
  0.0 78.4 jit_solution(15260410879058258898)
XLA Ops:
  0.0 0.8 select_reduce_fusion.1
  0.8 0.1 fusion.13
  0.9 0.2 reduce_window_sum.11
  1.0 0.2 select_reduce_fusion
  1.2 1.0 %scatter_custom_fusion = s32[256]{0:T(256)S(1)} fusion(s32[128]{0:T(128)S(1)} %fusion.14, s32[128]{0:T(128)S(1)} %iota.24, s32[]{:T(128)} %constant.11.clone.1), kind=kCustom, calls=%fused_computation.35 | custom fusion | bytes 1028 | tf_op jit(solution)/shard_map/scatter | solution.py:37
  2.2 1.9 %gather_fusion = s32[256]{0:T(256)S(1)} fusion(s32[128]{0:T(128)} %param.4, s32[1024]{0:T(1024)S(1)} %pad_clamp_fusion.1), kind=kCustom, calls=%fused_computation | custom fusion | bytes 3072 | tf_op jit(solution)/shard_map/gather | solution.py:43
  4.1 0.1 broadcast_in_dim.67
  4.2 0.6 broadcast_in_dim.68
  4.9 11.5 %all-to-all-start = ((s32[128,1,8]{2,1,0:T(1,128)}), s32[128,1,8]{2,1,0:T(1,128)S(1)}, u32[]{:S(2)}, u32[]{:S(2)}) async-start(s32[128,1,8]{2,1,0:T(1,128)} %bitcast.2), calls=%async_computation | async-start | bytes 131072 | tf_op jit(solution)/shard_map/all_to_all | solution.py:53
  16.4 1.1 %fusion.9 = f32[128]{0:T(128)S(1)} fusion(bf16[128,1024]{1,0:T(8,128)(2,1)} %param.3), kind=kLoop, calls=%fused_computation.12 | loop fusion | flops 393088 | bytes 262656 | tf_op jit(solution)/shard_map/reduce_sum | solution.py:27
  17.5 1.1 %fusion.10 = bf16[128,1024]{1,0:T(8,128)(2,1)S(1)} fusion(bf16[128,1024]{1,0:T(8,128)(2,1)} %param.3, f32[128]{0:T(128)S(1)} %add_rsqrt_fusion), kind=kLoop, calls=%fused_computation.13 | loop fusion | flops 393216 | bytes 524800 | tf_op jit(solution)/shard_map/convert_element_type | solution.py:27
  18.5 1.2 %gather_fusion.1 = bf16[256,1024]{1,0:T(8,128)(2,1)S(1)} fusion(bf16[128,1024]{1,0:T(8,128)(2,1)S(1)} %fusion.10, s32[1024]{0:T(1024)S(1)} %pad_clamp_fusion.1), kind=kCustom, calls=%fused_computation.1 | custom fusion | bytes 1049600 | tf_op jit(solution)/shard_map/gather | solution.py:40
  19.7 0.1 broadcast_in_dim.69
  19.8 0.1 bitcast_select_fusion
  19.9 6.1 %all-to-all-done = s32[128,1,8]{2,1,0:T(1,128)S(1)} async-done(((s32[128,1,8]{2,1,0:T(1,128)}), s32[128,1,8]{2,1,0:T(1,128)S(1)}, u32[]{:S(2)}, u32[]{:S(2)}) %all-to-all-start) | async-done | bytes 4128 | tf_op jit(solution)/shard_map/all_to_all | solution.py:53
  26.1 1.6 %broadcast_in_dim.72 = bf16[32,4,8,1024]{3,2,1,0:T(8,128)(2,1)} broadcast(bf16[32,8,1024]{2,1,0:T(8,128)(2,1)S(1)} %bitcast_select_fusion), dimensions={0,2,3} | broadcast | bytes 2621440 | tf_op jit(solution)/shard_map/broadcast_in_dim | solution.py:45
  27.7 4.2 %all-to-all-start.1 = ((bf16[128,8,1024]{2,1,0:T(8,128)(2,1)}), bf16[128,8,1024]{2,1,0:T(8,128)(2,1)S(1)}, u32[]{:S(2)}, u32[]{:S(2)}) async-start(bf16[128,8,1024]{2,1,0:T(8,128)(2,1)} %bitcast.5), calls=%async_computation.1 | async-start | bytes 4194304 | tf_op jit(solution)/shard_map/all_to_all | solution.py:52
  32.0 0.1 iota_add_fusion
  32.0 0.1 add.92
  32.1 0.5 broadcast.118
  32.6 0.8 %reduce.6 = s32[128,8]{1,0:T(8,128)S(1)} reduce(s32[128,1,8]{2,1,0:T(1,128)S(1)} %all-to-all-done, s32[]{:T(128)} %broadcast.118), dimensions={1}, to_apply=%all_to_all.16.reduce_sub_computation.3 | reduce | bytes 8196 | tf_op jit(solution)/shard_map/all_to_all | solution.py:53
  33.4 0.1 eq.51
  33.6 0.1 eq.49
  33.7 29.1 %all-to-all-done.1 = bf16[128,8,1024]{2,1,0:T(8,128)(2,1)S(1)} async-done(((bf16[128,8,1024]{2,1,0:T(8,128)(2,1)}), bf16[128,8,1024]{2,1,0:T(8,128)(2,1)S(1)}, u32[]{:S(2)}, u32[]{:S(2)}) %all-to-all-start.1) | async-done | bytes 2097184 | tf_op jit(solution)/shard_map/all_to_all | solution.py:52
  62.8 1.0 %fusion.5 = f32[256]{0:T(256)S(1)} fusion(bf16[128,8,1024]{2,1,0:T(8,128)(2,1)S(1)} %all-to-all-done.1, bf16[32,4,8,1024]{3,2,1,0:T(8,128)(2,1)S(1)} %bitcast.24, s32[]{:T(128)S(6)} %select_n.42, s32[256]{0:T(256)S(1)} %add.92, s32[1024]{0:T(1024)S(1)} %eq.51, s32[256]{0:T(256)S(1)} %eq.49, pred[1024]{0:T(1024)(128)(4,1)S(1)} %broadcast_compare_fusion), kind=kOutput, calls=%fused_computation.7 | convolution fusion | flops 538443520 | bytes 2629636 | tf_op jit(solution)/shard_map/dot_general | solution.py:8
  63.7 0.7 all_to_all.18
  64.4 3.9 %all-to-all-start.2 = ((f32[32,1,8]{2,1,0:T(1,128)}), f32[32,1,8]{2,1,0:T(1,128)S(1)}, u32[]{:S(2)}, u32[]{:S(2)}) async-start(f32[32,1,8]{2,1,0:T(1,128)} %bitcast.9), calls=%async_computation.2 | async-start | bytes 32768 | tf_op jit(solution)/shard_map/all_to_all | solution.py:73
  68.3 7.0 %all-to-all-done.2 = f32[32,1,8]{2,1,0:T(1,128)S(1)} async-done(((f32[32,1,8]{2,1,0:T(1,128)}), f32[32,1,8]{2,1,0:T(1,128)S(1)}, u32[]{:S(2)}, u32[]{:S(2)}) %all-to-all-start.2) | async-done | bytes 1056 | tf_op jit(solution)/shard_map/all_to_all | solution.py:73
  75.4 0.5 broadcast.119
  75.9 0.7 reduce.7
  76.6 0.1 reshape.119
  76.7 1.8 %gather_fusion.2 = f32[128]{0:T(128)} fusion(f32[256]{0:T(256)S(1)} %reshape.119, s32[1024]{0:T(1024)S(1)} %pad_clamp_fusion), kind=kCustom, calls=%fused_computation.2 | custom fusion | bytes 1536 | tf_op jit(solution)/shard_map/gather | solution.py:76
  (10 shorter events, 0.1 us)
Async XLA Ops:
  4.9 21.2 %all-to-all-start = ((s32[128,1,8]{2,1,0:T(1,128)}), s32[128,1,8]{2,1,0:T(1,128)S(1)}, u32[]{:S(2)}, u32[]{:S(2)}) async-start(s32[128,1,8]{2,1,0:T(1,128)} %bitcast.2), calls=%async_computation | async-start | bytes 131072 | tf_op jit(solution)/shard_map/all_to_all | solution.py:53
  27.7 35.1 %all-to-all-start.1 = ((bf16[128,8,1024]{2,1,0:T(8,128)(2,1)}), bf16[128,8,1024]{2,1,0:T(8,128)(2,1)S(1)}, u32[]{:S(2)}, u32[]{:S(2)}) async-start(bf16[128,8,1024]{2,1,0:T(8,128)(2,1)} %bitcast.5), calls=%async_computation.1 | async-start | bytes 4194304 | tf_op jit(solution)/shard_map/all_to_all | solution.py:52
  64.4 11.0 %all-to-all-start.2 = ((f32[32,1,8]{2,1,0:T(1,128)}), f32[32,1,8]{2,1,0:T(1,128)S(1)}, u32[]{:S(2)}, u32[]{:S(2)}) async-start(f32[32,1,8]{2,1,0:T(1,128)} %bitcast.9), calls=%async_computation.2 | async-start | bytes 32768 | tf_op jit(solution)/shard_map/all_to_all | solution.py:73
where the time goes:
time: 78.8 us; the launch traced here: 78.4 us
  waiting for transfers between devices  42.3 us (54%)
  starting transfers between devices  19.6 us (25%)
  local copies, waits for them, and re-layouts  10.3 us (13%)
  other arithmetic  5.07 us (6%)
  matrix products  0.95 us (1%)
    all_to_all x1, waiting for transfers between devices, on_device(): lax.all_to_all(wide_rows, ('owner', 'split'), split_axis=0, concat_axis=0...  29.1 us
    all_to_all x1, starting transfers between devices, on_device(): lax.all_to_all(wide_labels, ('owner', 'split'), split_axis=0, concat_axis...  11.5 us
    all_to_all x1, waiting for transfers between devices, on_device(): lax.all_to_all(best.reshape(owners, capacity), 'owner', split_axis=0, con...  7.04 us
    all_to_all x1, waiting for transfers between devices, on_device(): lax.all_to_all(wide_labels, ('owner', 'split'), split_axis=0, concat_axis...  6.14 us
    all_to_all x1, starting transfers between devices, on_device(): lax.all_to_all(wide_rows, ('owner', 'split'), split_axis=0, concat_axis=0...  4.25 us
    all_to_all x1, starting transfers between devices, on_device(): lax.all_to_all(best.reshape(owners, capacity), 'owner', split_axis=0, con...  3.9 us
    gather x1, local copies, waits for them, and re-layouts, on_device(): cluster[picked]  1.89 us
    gather x1, local copies, waits for them, and re-layouts, on_device(): return returned.reshape(held)[slot]  1.77 us
  transfers between devices with their start and end apart: 3, of which 3 were waited for; matrix products, arithmetic and copies ran while one was open for 7% of the time, Pallas kernels for 0%

commit v1 on v0

v1 whole, which is shorter than its diff:
```python
import functools

import jax
import jax.numpy as jnp
from jax import lax
from jax.experimental import pallas as pl
from jax.experimental.pallas import tpu as pltpu
from jax.sharding import PartitionSpec as P

MESH = pl.DeviceIdType.MESH
OWNERS = 32
SPLITS = 4
CAP = 8
WIDTH = 1024
HALF = WIDTH // 2
ROWS = 128
CLUSTERS = 64
GROUPS = 4
GROUP_ROWS = 256
STEPS_PER_GROUP = OWNERS // GROUPS
MULT = 1
INV = pow(MULT, -1, 32)
STAGES = 9


def place_of(owner):
    return ((owner // 2) % 4 + owner // 8 + 2 * (owner % 2)) % SPLITS


def kernel(
    emb_ref, clu_ref, own_ref, out_ref,
    send, lab_send, recv, lab_recv, held, best, ret_recv,
    send_sem, lab_send_sem, ret_send_sem, recv_sem, lab_sem, ret_sem,
):
    me = lax.axis_index("owner")
    split = lax.axis_index("split")
    is_owner = place_of(me) == split
    barrier = pltpu.get_barrier_semaphore()

    @pl.when(is_owner)
    def _():
        def greet(p, c):
            pl.semaphore_signal(
                barrier, inc=1, device_id=((me + p // SPLITS) % OWNERS, (split + p) % SPLITS),
                device_id_type=MESH,
            )
            return c
        lax.fori_loop(1, OWNERS * SPLITS, greet, 0)

    cluster = clu_ref[...]
    hot = (lax.broadcasted_iota(jnp.int32, (CLUSTERS, ROWS), 0) == cluster).astype(jnp.bfloat16)
    table = (lax.broadcasted_iota(jnp.int32, (OWNERS, CLUSTERS), 0) == own_ref[...]).astype(jnp.bfloat16)
    owner_hot = jnp.dot(table, hot, preferred_element_type=jnp.float32)
    before = (
        lax.broadcasted_iota(jnp.int32, (ROWS, ROWS), 0) < lax.broadcasted_iota(jnp.int32, (ROWS, ROWS), 1)
    ).astype(jnp.bfloat16)
    count = jnp.dot(owner_hot.astype(jnp.bfloat16), before, preferred_element_type=jnp.float32)
    rank = jnp.sum(owner_hot * count, 0, keepdims=True).astype(jnp.int32)
    owner_id = lax.broadcasted_iota(jnp.int32, (OWNERS, ROWS), 0)
    step_id = ((owner_id - me + OWNERS) * INV) & (OWNERS - 1)
    step = jnp.sum(owner_hot * step_id.astype(jnp.float32), 0, keepdims=True).astype(jnp.int32)
    lane = ((step & 3) * SPLITS + split) * CAP + rank
    lane_hot = lax.broadcasted_iota(jnp.int32, (ROWS, ROWS), 0) == lane
    step_hot = lax.broadcasted_iota(jnp.int32, (OWNERS, ROWS), 0) == step
    step_labels = jnp.where(step_hot, (cluster + 1).astype(jnp.float32), 0.0).astype(jnp.bfloat16)
    lab_send[...] = lax.dot_general(
        step_labels, lane_hot.astype(jnp.bfloat16), (((1,), (1,)), ((), ())),
        preferred_element_type=jnp.float32,
    )
    values = emb_ref[...].astype(jnp.float32)
    unit = (values * lax.rsqrt(jnp.sum(values * values, 1, keepdims=True) + 1e-06)).astype(jnp.bfloat16)
    pick = (
        lax.broadcasted_iota(jnp.int32, (OWNERS * CAP, ROWS), 0) == step * CAP + rank
    ).astype(jnp.bfloat16)
    for h in range(2):
        rows = jnp.dot(pick, unit[:, h * HALF:(h + 1) * HALF], preferred_element_type=jnp.float32)
        if h == 0:
            low = rows.reshape(OWNERS, CAP, HALF)
        else:
            send[...] = jnp.concatenate([low, rows.reshape(OWNERS, CAP, HALF)], 1).astype(jnp.bfloat16)

    @pl.when(is_owner)
    def _():
        pl.semaphore_wait(barrier, OWNERS - 1)

    @pl.when(jnp.logical_not(is_owner))
    def _():
        pl.semaphore_wait(barrier, OWNERS)

    if STAGES >= 2:
        def post(t, c):
            to = (me + MULT * t) % OWNERS
            there = place_of(to)
            p = t * SPLITS + split
            remote = jnp.logical_not((to == me) & (there == split))

            @pl.when(remote)
            def _():
                pltpu.make_async_remote_copy(
                    src_ref=lab_send.at[pl.ds(t, 1)], dst_ref=lab_recv.at[pl.ds(p, 1)],
                    send_sem=lab_send_sem, recv_sem=lab_sem,
                    device_id=(to, there), device_id_type=MESH,
                ).start()
                pltpu.make_async_remote_copy(
                    src_ref=send.at[t], dst_ref=recv.at[p],
                    send_sem=send_sem, recv_sem=recv_sem.at[t // STEPS_PER_GROUP],
                    device_id=(to, there), device_id_type=MESH,
                ).start()
            return c
        lax.fori_loop(0, OWNERS, post, 0)

    @pl.when(is_owner)
    def _():
        if STAGES >= 2:
            recv[split] = send[0]
            lab_recv[pl.ds(split, 1)] = lab_send[0:1]
            per = STEPS_PER_GROUP * SPLITS
            pltpu.make_async_copy(lab_recv.at[pl.ds(1, 127)], lab_recv.at[pl.ds(1, 127)], lab_sem).wait()
            labels = jnp.sum(lab_recv[...].reshape(8, 16, 128), 1)
            eye = (
                lax.broadcasted_iota(jnp.int32, (ROWS, ROWS), 0) == lax.broadcasted_iota(jnp.int32, (ROWS, ROWS), 1)
            )
            columns = lax.dot_general(
                eye.astype(jnp.bfloat16), labels.astype(jnp.bfloat16), (((1,), (1,)), ((), ())),
                preferred_element_type=jnp.float32,
            )
        if STAGES < 4:
            best[...] = jnp.zeros_like(best)
        if STAGES >= 2:
            tops = [None] * 8
            for g in range(GROUPS):
                if g == 0:
                    part = recv.at[pl.ds(0, per - 1)]
                else:
                    part = recv.at[pl.ds(g * per, per)]
                pltpu.make_async_copy(part, part, recv_sem.at[g]).wait()
                if STAGES >= 4:
                    got = recv[g * per:(g + 1) * per].astype(jnp.float32)
                    held[g * GROUP_ROWS:(g + 1) * GROUP_ROWS, :HALF] = (
                        got[:, :CAP].reshape(GROUP_ROWS, HALF).astype(jnp.bfloat16)
                    )
                    held[g * GROUP_ROWS:(g + 1) * GROUP_ROWS, HALF:] = (
                        got[:, CAP:].reshape(GROUP_ROWS, HALF).astype(jnp.bfloat16)
                    )
                    for a in range(g + 1):
                        for b in ([g] if a == g else [g, -1]):
                            i, j = (a, g) if b == g else (g, a)
                            scores = lax.dot_general(
                                held[i * GROUP_ROWS:(i + 1) * GROUP_ROWS, :],
                                held[j * GROUP_ROWS:(j + 1) * GROUP_ROWS, :],
                                (((1,), (1,)), ((), ())), preferred_element_type=jnp.float32,
                            )
                            for u in range(2):
                                for v in range(2):
                                    bi, bj = 2 * i + u, 2 * j + v
                                    same = columns[:, bi:bi + 1] == labels[bj:bj + 1, :]
                                    if bi == bj:
                                        same = same & jnp.logical_not(eye)
                                    top = jnp.max(
                                        jnp.where(
                                            same, scores[u * 128:(u + 1) * 128, v * 128:(v + 1) * 128], -2.0
                                        ), 0, keepdims=True,
                                    )
                                    tops[bj] = top if tops[bj] is None else jnp.maximum(tops[bj], top)
            if STAGES >= 4:
                for b in range(8):
                    best[b:b + 1, :] = tops[b]
        if STAGES >= 3:
            def give(p, c):
                to = (me - MULT * (p // SPLITS) + OWNERS * MULT) % OWNERS
                there = p % SPLITS
                remote = jnp.logical_not((to == me) & (there == split))

                @pl.when(remote)
                def _():
                    pltpu.make_async_remote_copy(
                        src_ref=best.at[pl.ds(p // 16, 1)], dst_ref=ret_recv.at[pl.ds(me, 1)],
                        send_sem=ret_send_sem, recv_sem=ret_sem,
                        device_id=(to, there), device_id_type=MESH,
                    ).start()
                return c
            lax.fori_loop(0, OWNERS * SPLITS, give, 0)
            ret_recv[pl.ds(me, 1)] = best[0:1]
            pltpu.make_async_copy(
                ret_recv.at[pl.ds(0, OWNERS - 1)], ret_recv.at[pl.ds(0, OWNERS - 1)], ret_sem
            ).wait()
            pltpu.make_async_copy(lab_recv.at[pl.ds(0, 127)], lab_recv.at[pl.ds(0, 127)], ret_send_sem).wait()
        if STAGES >= 2:
            pltpu.make_async_copy(send.at[pl.ds(0, OWNERS - 1)], send.at[pl.ds(0, OWNERS - 1)], send_sem).wait()
            pltpu.make_async_copy(
                lab_send.at[pl.ds(0, OWNERS - 1)], lab_send.at[pl.ds(0, OWNERS - 1)], lab_send_sem
            ).wait()

    @pl.when(jnp.logical_not(is_owner))
    def _():
        if STAGES >= 3:
            pltpu.make_async_copy(ret_recv, ret_recv, ret_sem).wait()
        if STAGES >= 2:
            pltpu.make_async_copy(send, send, send_sem).wait()
            pltpu.make_async_copy(lab_send, lab_send, lab_send_sem).wait()

    if STAGES >= 3:
        spread = lax.dot_general(
            ret_recv[...], owner_hot, (((0,), (0,)), ((), ())),
            precision=lax.Precision.HIGHEST, preferred_element_type=jnp.float32,
        )
        out_ref[...] = jnp.sum(jnp.where(lane_hot, spread, 0.0), 0, keepdims=True)
    else:
        out_ref[...] = jnp.sum(jnp.where(lane_hot, 1.0, 0.0), 0, keepdims=True)


def on_device(emb, cluster, owner_of):
    vmem = pl.BlockSpec(memory_space=pltpu.VMEM)
    best = pl.pallas_call(
        kernel,
        out_shape=jax.ShapeDtypeStruct((1, ROWS), jnp.float32),
        in_specs=[vmem] * 3,
        out_specs=vmem,
        scratch_shapes=[
            pltpu.VMEM((OWNERS, 2 * CAP, HALF), jnp.bfloat16),
            pltpu.VMEM((OWNERS, 128), jnp.float32),
            pltpu.VMEM((OWNERS * SPLITS, 2 * CAP, HALF), jnp.bfloat16),
            pltpu.VMEM((OWNERS * SPLITS, 128), jnp.float32),
            pltpu.VMEM((OWNERS * SPLITS * CAP, WIDTH), jnp.bfloat16),
            pltpu.VMEM((8, 128), jnp.float32),
            pltpu.VMEM((OWNERS, 128), jnp.float32),
            pltpu.SemaphoreType.DMA,
            pltpu.SemaphoreType.DMA,
            pltpu.SemaphoreType.DMA,
            pltpu.SemaphoreType.DMA((GROUPS,)),
            pltpu.SemaphoreType.DMA,
            pltpu.SemaphoreType.DMA,
        ],
        compiler_params=pltpu.CompilerParams(
            collective_id=0, has_side_effects=True, vmem_limit_bytes=32 * 1024 * 1024
        ),
    )(emb, cluster.reshape(1, ROWS), owner_of.reshape(1, CLUSTERS))
    return best.reshape(ROWS)


def solution(mesh):
    return jax.shard_map(
        on_device,
        mesh=mesh,
        in_specs=(P(("owner", "split"), None), P(("owner", "split")), P()),
        out_specs=P(("owner", "split")),
        check_vma=False,
    )
```

time: 78.8 us -> 38.9 us (0.49)
  waiting for transfers between devices: 42.3 us -> 0 us
  Pallas kernels: 0 us -> 36.6 us
  starting transfers between devices: 19.6 us -> 0 us
  local copies, waits for them, and re-layouts: 10.3 us -> 2.13 us
  other arithmetic: 5.07 us -> 0 us
  matrix products: 0.95 us -> 0 us
    all_to_all x3 -> x0, waiting for transfers between devices: 42.3 us -> none  [the longest x1 29.1 us: on_device(): lax.all_to_all(wide_rows, ('owner', 'split'), split_axis=0, concat_axis=0...]
    pallas_call x0 -> x1, Pallas kernels: none -> 36.6 us  [on_device(): pl.pallas_call(kernel, out_shape=jax.ShapeDtypeStruct((1, ROWS), jnp.floa...]
    all_to_all x3 -> x0, starting transfers between devices: 19.6 us -> none  [the longest x1 11.5 us: on_device(): lax.all_to_all(wide_labels, ('owner', 'split'), split_axis=0, concat_axis...]
    gather x3 -> x0, local copies, waits for them, and re-layouts: 4.83 us -> none  [the longest x1 1.89 us: on_device(): cluster[picked]]
    broadcast_in_dim x4 -> x0, local copies, waits for them, and re-layouts: 2.43 us -> none  [the longest x1 1.62 us: on_device(): jnp.broadcast_to(send_rows[:, None], (owners, splits, capacity, width))]
    unnamed x0 -> x7, local copies, waits for them, and re-layouts: none -> 2.13 us
    reduce_sum x3 -> x0, other arithmetic: 2.02 us -> none  [the longest x1 1.08 us: on_device(): jnp.sum(values * values, 1, keepdims=True) + 1e-06]
    all_to_all x3 -> x0, local copies, waits for them, and re-layouts: 1.72 us -> none  [the longest x2 1.2 us: on_device(): lax.all_to_all(best.reshape(owners, capacity), 'owner', split_axis=0, con...]
  transfers between devices with their start and end apart: 3 -> 0, of which waited for: 3 -> 0; matrix products, arithmetic and copies ran while one was open for 7% -> 0% of each run, Pallas kernels for 0% -> 0%
where the time goes in v1:
time: 38.9 us; the launch traced here: 38.7 us
  Pallas kernels  36.6 us (94%)
  local copies, waits for them, and re-layouts  2.13 us (5%)
    pallas_call x1, Pallas kernels, on_device(): pl.pallas_call(kernel, out_shape=jax.ShapeDtypeStruct((1, ROWS), jnp.floa...  36.6 us
    unnamed x7, local copies, waits for them, and re-layouts  2.13 us

profile of v1, /device:TPU:1, one launch (start us, length us, event | category | flops | bytes accessed | tf_op | source)
XLA Modules:
  0.0 38.7 jit_solution(1349995678098097647)
XLA Ops:
  0.0 0.0 copy-start.1
  0.0 0.0 copy-start.2
  0.0 0.7 %copy-done.1 = s32[128]{0:T(128)S(1)} copy-done((s32[128]{0:T(128)S(1)}, s32[128]{0:T(128)}, u32[]{:S(2)}) %copy-start.1) | copy-done | bytes 536
  0.7 0.0 copy-done.2
  0.7 0.0 copy-start
  0.7 0.9 %copy-done = bf16[128,1024]{1,0:T(8,128)(2,1)S(1)} copy-done((bf16[128,1024]{1,0:T(8,128)(2,1)S(1)}, bf16[128,1024]{1,0:T(8,128)(2,1)}, u32[]{:S(2)}) %copy-start) | copy-done | bytes 262168
  1.6 36.6 %shard_map.37 = f32[1,128]{1,0:T(1,128)S(1)} custom-call(bf16[128,1024]{1,0:T(8,128)(2,1)S(1)} %copy-done, s32[1,128]{1,0:T(1,128)S(1)} %bitcast.3, s32[1,64]{1,0:T(1,128)S(1)} %bitcast.4), custom_call_target="tpu_custom_call" | custom-call | tf_op jit(solution)/shard_map/pallas_call | solution.py:214
  38.2 0.5 %copy.5 = f32[128]{0:T(128)} copy(f32[128]{0:T(128)S(1)} %bitcast.5) | data formatting | bytes 1024
Async XLA Ops:
  0.0 0.7 %copy-start.1 = (s32[128]{0:T(128)S(1)}, s32[128]{0:T(128)}, u32[]{:S(2)}) copy-start(s32[128]{0:T(128)} %param.4) | copy-start | bytes 1540
  0.0 0.7 %copy-start.2 = (s32[64]{0:T(128)S(1)}, s32[64]{0:T(128)}, u32[]{:S(2)}) copy-start(s32[64]{0:T(128)} %param.5) | copy-start | bytes 772
  0.7 0.9 %copy-start = (bf16[128,1024]{1,0:T(8,128)(2,1)S(1)}, bf16[128,1024]{1,0:T(8,128)(2,1)}, u32[]{:S(2)}) copy-start(bf16[128,1024]{1,0:T(8,128)(2,1)} %emb_ref.1) | copy-start | bytes 786436

commit v2 on v0

v2 whole, which is shorter than its diff:
```python
import jax
import jax.numpy as jnp
from jax import lax
from jax.experimental import pallas as pl
from jax.experimental.pallas import tpu as pltpu
from jax.sharding import PartitionSpec as P

MESH = pl.DeviceIdType.MESH
OWNERS = 32
SPLITS = 4
CAP = 8
WIDTH = 1024
HALF = WIDTH // 2
ROWS = 128
CLUSTERS = 64
DEVICES = OWNERS * SPLITS
GROUPS = 4
PER = DEVICES // GROUPS
GROUP_ROWS = PER * CAP
CORE = 1
VL = 24
STAGES = 9
MULT = 1
ORDER = 1
FLIP = 0
SPIN_X = 1
SPIN_M = 1
UNROLL = 4


def home_of(o):
    return lax.div(o, 4) * 2 + CORE, lax.rem(o, 4)


def owner_at(me, split):
    return (lax.rem(me, 2) == CORE) & (me < 16), lax.rem(lax.div(me, 2), 8) * 4 + split


def spot_of(z, y, core):
    if ORDER == 0:
        return z * 32 + core * 16 + y * 4
    return core * 64 + z * 16 + y * 4


def iota(shape, dim):
    return lax.broadcasted_iota(jnp.int32, shape, dim)


def wait_bytes(ref, sem):
    pltpu.make_async_copy(ref, ref, sem).wait()


def kernel(
    emb_hbm, clu_hbm, own_hbm, out_ref,
    emb_ref, clu_ref, own_ref, send, lab_send, recv, lab_recv, held, best, ret_recv,
    load_sem, send_sem, lab_send_sem, ret_send_sem, recv_sem, lab_sem, ret_sem,
):
    me = lax.axis_index("owner")
    split = lax.axis_index("split")
    is_owner, mine = owner_at(me, split)
    z, y, core = lax.div(me, 8), lax.rem(lax.div(me, 2), 4), lax.rem(me, 2)
    here = spot_of(z, y, core) + split
    loads = [
        pltpu.make_async_copy(src, dst, load_sem.at[i])
        for i, (src, dst) in enumerate(((clu_hbm, clu_ref), (own_hbm, own_ref), (emb_hbm, emb_ref)))
    ]
    for load in loads:
        load.start()
    barrier = pltpu.get_barrier_semaphore()

    @pl.when(is_owner)
    def _():
        for q in range(1, SPLITS):
            pl.semaphore_signal(
                barrier, inc=1, device_id=(me, lax.rem(split + q, SPLITS)), device_id_type=MESH
            )

        def greet(t, c):
            to = lax.rem(me + OWNERS - t, OWNERS)
            for q in range(SPLITS):
                pl.semaphore_signal(barrier, inc=1, device_id=(to, q), device_id_type=MESH)
            return c
        lax.fori_loop(1, OWNERS, greet, 0, unroll=UNROLL)

    loads[0].wait()
    loads[1].wait()
    cluster = clu_ref[...]
    hot = (iota((CLUSTERS, ROWS), 0) == cluster).astype(jnp.bfloat16)
    table = (iota((OWNERS, CLUSTERS), 0) == own_ref[...]).astype(jnp.bfloat16)
    owner_hot = jnp.dot(table, hot, preferred_element_type=jnp.float32)
    before = (iota((ROWS, ROWS), 0) < iota((ROWS, ROWS), 1)).astype(jnp.bfloat16)
    count = jnp.dot(owner_hot.astype(jnp.bfloat16), before, preferred_element_type=jnp.float32)
    slot = jnp.sum(
        owner_hot * (count + CAP * iota((OWNERS, ROWS), 0).astype(jnp.float32)), 0, keepdims=True
    ).astype(jnp.int32)
    rank = slot & (CAP - 1)
    lane_hot = iota((ROWS, ROWS), 0) == lax.rem(here, 16) * CAP + rank
    labels = (owner_hot * (cluster + 1).astype(jnp.float32)).astype(jnp.bfloat16)
    lab_send[...] = lax.dot_general(
        labels, lane_hot.astype(jnp.bfloat16), (((1,), (1,)), ((), ())),
        preferred_element_type=jnp.float32,
    )
    loads[2].wait()
    values = emb_ref[...].astype(jnp.float32)
    unit = (values * lax.rsqrt(jnp.sum(values * values, 1, keepdims=True) + 1e-06)).astype(jnp.bfloat16)
    pick = (iota((OWNERS * CAP, ROWS), 0) == slot).astype(jnp.bfloat16)
    parts = [
        jnp.dot(pick, unit[:, h * HALF:(h + 1) * HALF], preferred_element_type=jnp.float32).reshape(
            OWNERS, CAP, HALF
        )
        for h in range(2)
    ]
    send[...] = jnp.concatenate(parts, 1).astype(jnp.bfloat16)

    @pl.when(is_owner)
    def _():
        pl.semaphore_wait(barrier, OWNERS - 1)

    @pl.when(jnp.logical_not(is_owner))
    def _():
        pl.semaphore_wait(barrier, OWNERS)

    group = lax.div(here, PER)

    def send_step(o):
        there = home_of(o)
        pltpu.make_async_remote_copy(
            src_ref=lab_send.at[pl.ds(o, 1)], dst_ref=lab_recv.at[pl.ds(here, 1)],
            send_sem=lab_send_sem, recv_sem=lab_sem, device_id=there, device_id_type=MESH,
        ).start()
        pltpu.make_async_remote_copy(
            src_ref=send.at[o], dst_ref=recv.at[here],
            send_sem=send_sem, recv_sem=recv_sem.at[group], device_id=there, device_id_type=MESH,
        ).start()

    first = lax.rem(SPIN_X * split + SPIN_M * me, OWNERS)

    def post(t, c):
        o = lax.rem(first + MULT * t, OWNERS)

        @pl.when(jnp.logical_not(is_owner & (o == mine)))
        def _():
            send_step(o)
        return c
    if STAGES >= 2:
        lax.fori_loop(0, OWNERS, post, 0, unroll=UNROLL)

    @pl.when(is_owner)
    def _():
        if STAGES >= 2:
            recv[here] = send[mine]
            lab_recv[pl.ds(here, 1)] = lab_send[pl.ds(mine, 1)]
            wait_bytes(lab_recv.at[pl.ds(0, DEVICES - 1)], lab_sem)
            labels = jnp.sum(lab_recv[...].reshape(8, 16, 128), 1)
            eye = iota((ROWS, ROWS), 0) == iota((ROWS, ROWS), 1)
            columns = lax.dot_general(
                eye.astype(jnp.bfloat16), labels.astype(jnp.bfloat16), (((1,), (1,)), ((), ())),
                preferred_element_type=jnp.float32,
            )
            tops, wides = [None] * 8, [None] * 6
            for g in range(GROUPS):
                @pl.when(group == g)
                def _():
                    wait_bytes(recv.at[pl.ds(0, PER - 1)], recv_sem.at[g])

                @pl.when(group != g)
                def _():
                    wait_bytes(recv.at[pl.ds(0, PER)], recv_sem.at[g])
                if STAGES < 4:
                    continue
                got = recv[g * PER:(g + 1) * PER].astype(jnp.float32)
                for h in range(2):
                    held[g * GROUP_ROWS:(g + 1) * GROUP_ROWS, h * HALF:(h + 1) * HALF] = (
                        got[:, h * CAP:(h + 1) * CAP].reshape(GROUP_ROWS, HALF).astype(jnp.bfloat16)
                    )
                seen = (g + 1) * GROUP_ROWS
                scores = lax.dot_general(
                    held[0:seen, :], held[g * GROUP_ROWS:seen, :], (((1,), (1,)), ((), ())),
                    preferred_element_type=jnp.float32,
                )
                for bi in range(2 * g + 2):
                    wide = None
                    for v in range(2):
                        bj = 2 * g + v
                        same = columns[:, bi:bi + 1] == labels[bj:bj + 1, :]
                        if bi == bj:
                            same = same & jnp.logical_not(eye)
                        kept = jnp.where(same, scores[bi * 128:(bi + 1) * 128, v * 128:(v + 1) * 128], -2.0)
                        top = jnp.max(kept, 0, keepdims=True)
                        tops[bj] = top if tops[bj] is None else jnp.maximum(tops[bj], top)
                        wide = kept if wide is None else jnp.maximum(wide, kept)
                    if bi < 2 * g:
                        wides[bi] = wide if wides[bi] is None else jnp.maximum(wides[bi], wide)
            if STAGES >= 4:
                for b in range(6):
                    if FLIP == 0:
                        top = jnp.max(jnp.transpose(wides[b]), 0, keepdims=True)
                    else:
                        col = jnp.max(wides[b], 1, keepdims=True)
                        top = jnp.max(jnp.where(eye, col, -2.0), 0, keepdims=True)
                    tops[b] = jnp.maximum(tops[b], top)
            for b in range(8):
                best[b:b + 1, :] = tops[b] if STAGES >= 4 else jnp.zeros((1, 128), jnp.float32)
        if STAGES >= 3:
            def give(m, c):
                for q in range(SPLITS):
                    @pl.when(jnp.logical_not((m == me) & (q == split)))
                    def _():
                        pltpu.make_async_remote_copy(
                            src_ref=best.at[pl.ds(lax.div(spot_of(lax.div(m, 8), lax.rem(lax.div(m, 2), 4), lax.rem(m, 2)), 16), 1)], dst_ref=ret_recv.at[pl.ds(mine, 1)],
                            send_sem=ret_send_sem, recv_sem=ret_sem,
                            device_id=(m, q), device_id_type=MESH,
                        ).start()
                return c
            lax.fori_loop(0, OWNERS, give, 0, unroll=UNROLL)
            ret_recv[pl.ds(mine, 1)] = best[pl.ds(lax.div(here, 16), 1)]
            wait_bytes(ret_recv.at[pl.ds(0, OWNERS - 1)], ret_sem)

    if STAGES >= 3:
        @pl.when(jnp.logical_not(is_owner))
        def _():
            wait_bytes(ret_recv, ret_sem)
        rest = ret_recv[...]
        terms = []
        for _ in range(3):
            terms.append(rest.astype(jnp.bfloat16))
            rest = rest - terms[-1].astype(jnp.float32)
        spread = lax.dot_general(
            jnp.concatenate(terms, 0), jnp.concatenate([owner_hot.astype(jnp.bfloat16)] * 3, 0),
            (((0,), (0,)), ((), ())), preferred_element_type=jnp.float32,
        )
        out_ref[...] = jnp.sum(jnp.where(lane_hot, spread, 0.0), 0, keepdims=True)
    else:
        out_ref[...] = jnp.sum(jnp.where(lane_hot, 1.0, 0.0), 0, keepdims=True)

    @pl.when(is_owner)
    def _():
        wait_bytes(send.at[pl.ds(0, OWNERS - 1)], send_sem)
        wait_bytes(lab_send.at[pl.ds(0, OWNERS - 1)], lab_send_sem)
        if STAGES >= 3:
            wait_bytes(lab_recv.at[pl.ds(0, DEVICES - 1)], ret_send_sem)

    @pl.when(jnp.logical_not(is_owner))
    def _():
        wait_bytes(send, send_sem)
        wait_bytes(lab_send, lab_send_sem)


def on_device(emb, cluster, owner_of):
    best = pl.pallas_call(
        kernel,
        out_shape=jax.ShapeDtypeStruct((1, ROWS), jnp.float32),
        in_specs=[pl.BlockSpec(memory_space=pltpu.HBM)] * 3,
        out_specs=pl.BlockSpec(memory_space=pltpu.VMEM),
        scratch_shapes=[
            pltpu.VMEM((ROWS, WIDTH), jnp.bfloat16),
            pltpu.VMEM((1, ROWS), jnp.int32),
            pltpu.VMEM((1, CLUSTERS), jnp.int32),
            pltpu.VMEM((OWNERS, 2 * CAP, HALF), jnp.bfloat16),
            pltpu.VMEM((OWNERS, 128), jnp.float32),
            pltpu.VMEM((DEVICES, 2 * CAP, HALF), jnp.bfloat16),
            pltpu.VMEM((DEVICES, 128), jnp.float32),
            pltpu.VMEM((DEVICES * CAP, WIDTH), jnp.bfloat16),
            pltpu.VMEM((8, 128), jnp.float32),
            pltpu.VMEM((OWNERS, 128), jnp.float32),
            pltpu.SemaphoreType.DMA((3,)),
            pltpu.SemaphoreType.DMA,
            pltpu.SemaphoreType.DMA,
            pltpu.SemaphoreType.DMA,
            pltpu.SemaphoreType.DMA((GROUPS,)),
            pltpu.SemaphoreType.DMA,
            pltpu.SemaphoreType.DMA,
        ],
        compiler_params=pltpu.CompilerParams(
            collective_id=0, has_side_effects=True, vmem_limit_bytes=VL * 1024 * 1024
        ),
    )(*[
        pltpu.with_memory_space_constraint(a, pltpu.HBM)
        for a in (emb, cluster.reshape(1, ROWS), owner_of.reshape(1, CLUSTERS))
    ])
    return best.reshape(ROWS)


def solution(mesh):
    return jax.shard_map(
        on_device,
        mesh=mesh,
        in_specs=(P(("owner", "split"), None), P(("owner", "split")), P()),
        out_specs=P(("owner", "split")),
        check_vma=False,
    )
```

time: 78.8 us -> 29.8 us (0.38)
  waiting for transfers between devices: 42.3 us -> 0 us
  Pallas kernels: 0 us -> 29.2 us
  starting transfers between devices: 19.6 us -> 0 us
  local copies, waits for them, and re-layouts: 10.3 us -> 0.51 us
  other arithmetic: 5.07 us -> 0 us
  matrix products: 0.95 us -> 0 us
    all_to_all x3 -> x0, waiting for transfers between devices: 42.3 us -> none  [the longest x1 29.1 us: on_device(): lax.all_to_all(wide_rows, ('owner', 'split'), split_axis=0, concat_axis=0...]
    pallas_call x0 -> x1, Pallas kernels: none -> 29.2 us  [on_device(): pl.pallas_call(kernel, out_shape=jax.ShapeDtypeStruct((1, ROWS), jnp.floa...]
    all_to_all x3 -> x0, starting transfers between devices: 19.6 us -> none  [the longest x1 11.5 us: on_device(): lax.all_to_all(wide_labels, ('owner', 'split'), split_axis=0, concat_axis...]
    gather x3 -> x0, local copies, waits for them, and re-layouts: 4.83 us -> none  [the longest x1 1.89 us: on_device(): cluster[picked]]
    broadcast_in_dim x4 -> x0, local copies, waits for them, and re-layouts: 2.43 us -> none  [the longest x1 1.62 us: on_device(): jnp.broadcast_to(send_rows[:, None], (owners, splits, capacity, width))]
    reduce_sum x3 -> x0, other arithmetic: 2.02 us -> none  [the longest x1 1.08 us: on_device(): jnp.sum(values * values, 1, keepdims=True) + 1e-06]
    all_to_all x3 -> x0, local copies, waits for them, and re-layouts: 1.72 us -> none  [the longest x2 1.2 us: on_device(): lax.all_to_all(best.reshape(owners, capacity), 'owner', split_axis=0, con...]
    all_to_all x2 -> x0, other arithmetic: 1.49 us -> none  [the longest x1 0.81 us: on_device(): lax.all_to_all(wide_labels, ('owner', 'split'), split_axis=0, concat_axis...]
  transfers between devices with their start and end apart: 3 -> 0, of which waited for: 3 -> 0; matrix products, arithmetic and copies ran while one was open for 7% -> 0% of each run, Pallas kernels for 0% -> 0%
where the time goes in v2:
time: 29.8 us; the launch traced here: 29.7 us
  Pallas kernels  29.2 us (98%)
  local copies, waits for them, and re-layouts  0.51 us (2%)
    pallas_call x1, Pallas kernels, on_device(): pl.pallas_call(kernel, out_shape=jax.ShapeDtypeStruct((1, ROWS), jnp.floa...  29.2 us

profile of v2, /device:TPU:1, one launch (start us, length us, event | category | flops | bytes accessed | tf_op | source)
XLA Modules:
  0.0 29.7 jit_solution(10546125329747415679)
XLA Ops:
  0.0 29.2 %shard_map.37 = f32[1,128]{1,0:T(1,128)S(1)} custom-call(bf16[128,1024]{1,0:T(8,128)(2,1)} %emb_hbm.1, s32[1,128]{1,0:T(1,128)} %bitcast.4, s32[1,64]{1,0:T(1,128)} %bitcast.5), custom_call_target="tpu_custom_call" | custom-call | tf_op jit(solution)/shard_map/pallas_call | solution.py:250
  29.2 0.5 %copy.5 = f32[128]{0:T(128)} copy(f32[128]{0:T(128)S(1)} %bitcast.3) | data formatting | bytes 1024

commit v3 on v2

--- a/solution.py
+++ b/solution.py
@@ -17,29 +17,15 @@
 GROUPS = 4
 PER = DEVICES // GROUPS
 GROUP_ROWS = PER * CAP
-CORE = 1
-VL = 24
 STAGES = 9
+UNROLL = 4
 MULT = 1
-ORDER = 1
-FLIP = 0
 SPIN_X = 1
 SPIN_M = 1
-UNROLL = 4
 
 
 def home_of(o):
-    return lax.div(o, 4) * 2 + CORE, lax.rem(o, 4)
-
-
-def owner_at(me, split):
-    return (lax.rem(me, 2) == CORE) & (me < 16), lax.rem(lax.div(me, 2), 8) * 4 + split
-
-
-def spot_of(z, y, core):
-    if ORDER == 0:
-        return z * 32 + core * 16 + y * 4
-    return core * 64 + z * 16 + y * 4
+    return lax.div(o, 4) * 2 + 1, lax.rem(o, 4)
 
 
 def iota(shape, dim):
@@ -57,9 +43,9 @@
 ):
     me = lax.axis_index("owner")
     split = lax.axis_index("split")
-    is_owner, mine = owner_at(me, split)
-    z, y, core = lax.div(me, 8), lax.rem(lax.div(me, 2), 4), lax.rem(me, 2)
-    here = spot_of(z, y, core) + split
+    here = me * SPLITS + split
+    is_owner = (lax.rem(me, 2) == 1) & (me < 16)
+    mine = lax.rem(lax.div(me, 2), 8) * 4 + split
     loads = [
         pltpu.make_async_copy(src, dst, load_sem.at[i])
         for i, (src, dst) in enumerate(((clu_hbm, clu_ref), (own_hbm, own_ref), (emb_hbm, emb_ref)))
@@ -70,17 +56,14 @@
 
     @pl.when(is_owner)
     def _():
-        for q in range(1, SPLITS):
-            pl.semaphore_signal(
-                barrier, inc=1, device_id=(me, lax.rem(split + q, SPLITS)), device_id_type=MESH
-            )
-
         def greet(t, c):
-            to = lax.rem(me + OWNERS - t, OWNERS)
+            to = OWNERS - 1 - t
             for q in range(SPLITS):
-                pl.semaphore_signal(barrier, inc=1, device_id=(to, q), device_id_type=MESH)
+                @pl.when(jnp.logical_not((to == me) & (q == split)))
+                def _():
+                    pl.semaphore_signal(barrier, inc=1, device_id=(to, q), device_id_type=MESH)
             return c
-        lax.fori_loop(1, OWNERS, greet, 0, unroll=UNROLL)
+        lax.fori_loop(0, OWNERS, greet, 0, unroll=UNROLL)
 
     loads[0].wait()
     loads[1].wait()
@@ -93,8 +76,7 @@
     slot = jnp.sum(
         owner_hot * (count + CAP * iota((OWNERS, ROWS), 0).astype(jnp.float32)), 0, keepdims=True
     ).astype(jnp.int32)
-    rank = slot & (CAP - 1)
-    lane_hot = iota((ROWS, ROWS), 0) == lax.rem(here, 16) * CAP + rank
+    lane_hot = iota((ROWS, ROWS), 0) == lax.rem(here, 16) * CAP + (slot & (CAP - 1))
     labels = (owner_hot * (cluster + 1).astype(jnp.float32)).astype(jnp.bfloat16)
     lab_send[...] = lax.dot_general(
         labels, lane_hot.astype(jnp.bfloat16), (((1,), (1,)), ((), ())),
@@ -111,28 +93,7 @@
         for h in range(2)
     ]
     send[...] = jnp.concatenate(parts, 1).astype(jnp.bfloat16)
-
-    @pl.when(is_owner)
-    def _():
-        pl.semaphore_wait(barrier, OWNERS - 1)
-
-    @pl.when(jnp.logical_not(is_owner))
-    def _():
-        pl.semaphore_wait(barrier, OWNERS)
-
-    group = lax.div(here, PER)
-
-    def send_step(o):
-        there = home_of(o)
-        pltpu.make_async_remote_copy(
-            src_ref=lab_send.at[pl.ds(o, 1)], dst_ref=lab_recv.at[pl.ds(here, 1)],
-            send_sem=lab_send_sem, recv_sem=lab_sem, device_id=there, device_id_type=MESH,
-        ).start()
-        pltpu.make_async_remote_copy(
-            src_ref=send.at[o], dst_ref=recv.at[here],
-            send_sem=send_sem, recv_sem=recv_sem.at[group], device_id=there, device_id_type=MESH,
-        ).start()
-
+    pl.semaphore_wait(barrier, jnp.where(is_owner, OWNERS - 1, OWNERS))
     first = lax.rem(SPIN_X * split + SPIN_M * me, OWNERS)
 
     def post(t, c):
@@ -140,7 +101,15 @@
 
         @pl.when(jnp.logical_not(is_owner & (o == mine)))
         def _():
-            send_step(o)
+            there = home_of(o)
+            pltpu.make_async_remote_copy(
+                src_ref=lab_send.at[pl.ds(o, 1)], dst_ref=lab_recv.at[pl.ds(here, 1)],
+                send_sem=lab_send_sem, recv_sem=lab_sem, device_id=there, device_id_type=MESH,
+            ).start()
+            pltpu.make_async_remote_copy(
+                src_ref=send.at[o], dst_ref=recv.at[here],
+                send_sem=send_sem, recv_sem=recv_sem, device_id=there, device_id_type=MESH,
+            ).start()
         return c
     if STAGES >= 2:
         lax.fori_loop(0, OWNERS, post, 0, unroll=UNROLL)
@@ -157,22 +126,15 @@
                 eye.astype(jnp.bfloat16), labels.astype(jnp.bfloat16), (((1,), (1,)), ((), ())),
                 preferred_element_type=jnp.float32,
             )
-            tops, wides = [None] * 8, [None] * 6
+            wait_bytes(recv.at[pl.ds(0, DEVICES - 1)], recv_sem)
+        tops, wides = [None] * 8, [None] * 6
+        if STAGES >= 4:
+            got = recv[...].astype(jnp.float32)
+            for h in range(2):
+                held[:, h * HALF:(h + 1) * HALF] = (
+                    got[:, h * CAP:(h + 1) * CAP].reshape(DEVICES * CAP, HALF).astype(jnp.bfloat16)
+                )
             for g in range(GROUPS):
-                @pl.when(group == g)
-                def _():
-                    wait_bytes(recv.at[pl.ds(0, PER - 1)], recv_sem.at[g])
-
-                @pl.when(group != g)
-                def _():
-                    wait_bytes(recv.at[pl.ds(0, PER)], recv_sem.at[g])
-                if STAGES < 4:
-                    continue
-                got = recv[g * PER:(g + 1) * PER].astype(jnp.float32)
-                for h in range(2):
-                    held[g * GROUP_ROWS:(g + 1) * GROUP_ROWS, h * HALF:(h + 1) * HALF] = (
-                        got[:, h * CAP:(h + 1) * CAP].reshape(GROUP_ROWS, HALF).astype(jnp.bfloat16)
-                    )
                 seen = (g + 1) * GROUP_ROWS
                 scores = lax.dot_general(
                     held[0:seen, :], held[g * GROUP_ROWS:seen, :], (((1,), (1,)), ((), ())),
@@ -191,23 +153,17 @@
                         wide = kept if wide is None else jnp.maximum(wide, kept)
                     if bi < 2 * g:
                         wides[bi] = wide if wides[bi] is None else jnp.maximum(wides[bi], wide)
-            if STAGES >= 4:
-                for b in range(6):
-                    if FLIP == 0:
-                        top = jnp.max(jnp.transpose(wides[b]), 0, keepdims=True)
-                    else:
-                        col = jnp.max(wides[b], 1, keepdims=True)
-                        top = jnp.max(jnp.where(eye, col, -2.0), 0, keepdims=True)
-                    tops[b] = jnp.maximum(tops[b], top)
-            for b in range(8):
-                best[b:b + 1, :] = tops[b] if STAGES >= 4 else jnp.zeros((1, 128), jnp.float32)
+            for b in range(6):
+                tops[b] = jnp.maximum(tops[b], jnp.max(jnp.transpose(wides[b]), 0, keepdims=True))
+        for b in range(8):
+            best[b:b + 1, :] = tops[b] if STAGES >= 4 else jnp.zeros((1, 128), jnp.float32)
         if STAGES >= 3:
             def give(m, c):
                 for q in range(SPLITS):
                     @pl.when(jnp.logical_not((m == me) & (q == split)))
                     def _():
                         pltpu.make_async_remote_copy(
-                            src_ref=best.at[pl.ds(lax.div(spot_of(lax.div(m, 8), lax.rem(lax.div(m, 2), 4), lax.rem(m, 2)), 16), 1)], dst_ref=ret_recv.at[pl.ds(mine, 1)],
+                            src_ref=best.at[pl.ds(lax.div(m, 4), 1)], dst_ref=ret_recv.at[pl.ds(mine, 1)],
                             send_sem=ret_send_sem, recv_sem=ret_sem,
                             device_id=(m, q), device_id_type=MESH,
                         ).start()
@@ -233,17 +189,18 @@
     else:
         out_ref[...] = jnp.sum(jnp.where(lane_hot, 1.0, 0.0), 0, keepdims=True)
 
-    @pl.when(is_owner)
-    def _():
-        wait_bytes(send.at[pl.ds(0, OWNERS - 1)], send_sem)
-        wait_bytes(lab_send.at[pl.ds(0, OWNERS - 1)], lab_send_sem)
-        if STAGES >= 3:
-            wait_bytes(lab_recv.at[pl.ds(0, DEVICES - 1)], ret_send_sem)
-
-    @pl.when(jnp.logical_not(is_owner))
-    def _():
-        wait_bytes(send, send_sem)
-        wait_bytes(lab_send, lab_send_sem)
+    if STAGES >= 2:
+        @pl.when(is_owner)
+        def _():
+            wait_bytes(send.at[pl.ds(0, OWNERS - 1)], send_sem)
+            wait_bytes(lab_send.at[pl.ds(0, OWNERS - 1)], lab_send_sem)
+            if STAGES >= 3:
+                wait_bytes(lab_recv.at[pl.ds(0, DEVICES - 1)], ret_send_sem)
+
+        @pl.when(jnp.logical_not(is_owner))
+        def _():
+            wait_bytes(send, send_sem)
+            wait_bytes(lab_send, lab_send_sem)
 
 
 def on_device(emb, cluster, owner_of):
@@ -267,12 +224,12 @@
             pltpu.SemaphoreType.DMA,
             pltpu.SemaphoreType.DMA,
             pltpu.SemaphoreType.DMA,
-            pltpu.SemaphoreType.DMA((GROUPS,)),
+            pltpu.SemaphoreType.DMA,
             pltpu.SemaphoreType.DMA,
             pltpu.SemaphoreType.DMA,
         ],
         compiler_params=pltpu.CompilerParams(
-            collective_id=0, has_side_effects=True, vmem_limit_bytes=VL * 1024 * 1024
+            collective_id=0, has_side_effects=True, vmem_limit_bytes=24 * 1024 * 1024
         ),
     )(*[
         pltpu.with_memory_space_constraint(a, pltpu.HBM)

time: 29.8 us -> 28.2 us (0.946)
  Pallas kernels: 29.2 us -> 27.5 us
    pallas_call x1, Pallas kernels: 29.2 us -> 27.5 us  [on_device(): pl.pallas_call(kernel, out_shape=jax.ShapeDtypeStruct((1, ROWS), jnp.floa...]
where the time goes in v3:
time: 28.2 us; the launch traced here: 28 us
  Pallas kernels  27.5 us (98%)
  local copies, waits for them, and re-layouts  0.51 us (2%)
    pallas_call x1, Pallas kernels, on_device(): pl.pallas_call(kernel, out_shape=jax.ShapeDtypeStruct((1, ROWS), jnp.floa...  27.5 us

profile of v3, /device:TPU:1, one launch (start us, length us, event | category | flops | bytes accessed | tf_op | source)
XLA Modules:
  0.0 28.0 jit_solution(10358140056241240529)
XLA Ops:
  0.0 27.5 %shard_map.37 = f32[1,128]{1,0:T(1,128)S(1)} custom-call(bf16[128,1024]{1,0:T(8,128)(2,1)} %emb_hbm.1, s32[1,128]{1,0:T(1,128)} %bitcast.4, s32[1,64]{1,0:T(1,128)} %bitcast.5), custom_call_target="tpu_custom_call" | custom-call | tf_op jit(solution)/shard_map/pallas_call | solution.py:207
  27.5 0.5 %copy.5 = f32[128]{0:T(128)} copy(f32[128]{0:T(128)S(1)} %bitcast.3) | data formatting | bytes 1024

commit v4 on v3

v4 whole, which is shorter than its diff:
```python
import jax
import jax.numpy as jnp
from jax import lax
from jax.experimental import pallas as pl
from jax.experimental.pallas import tpu as pltpu
from jax.sharding import PartitionSpec as P

MESH = pl.DeviceIdType.MESH
OWNERS = 32
SPLITS = 4
CAP = 8
WIDTH = 1024
HALF = WIDTH // 2
ROWS = 128
CLUSTERS = 64
DEVICES = OWNERS * SPLITS
GROUPS = 4
PER = DEVICES // GROUPS
GROUP_ROWS = PER * CAP
UNROLL = 4
MULT = 1
SPIN_X = 4
SPIN_M = 8


def home_of(o):
    return lax.div(o, 4) * 2 + 1, lax.rem(o, 4)


def iota(shape, dim):
    return lax.broadcasted_iota(jnp.int32, shape, dim)


def wait_bytes(ref, sem):
    pltpu.make_async_copy(ref, ref, sem).wait()


def kernel(
    emb_hbm, clu_hbm, own_hbm, out_ref,
    emb_ref, clu_ref, own_ref, send, lab_send, recv, lab_recv, held, soon, best, ret_recv,
    load_sem, send_sem, lab_send_sem, ret_send_sem, recv_sem, lab_sem, ret_sem,
):
    me = lax.axis_index("owner")
    split = lax.axis_index("split")
    z, y, core = lax.div(me, 8), lax.rem(lax.div(me, 2), 4), lax.rem(me, 2)
    here = (
        lax.div(z, 2) * 64 + lax.div(y, 2) * 32 + lax.div(split, 2) * 16
        + lax.rem(y, 2) * 8 + lax.rem(split, 2) * 4 + lax.rem(z, 2) * 2 + core
    )
    is_owner = (lax.rem(me, 2) == 1) & (me < 16)
    mine = lax.rem(lax.div(me, 2), 8) * 4 + split
    loads = [
        pltpu.make_async_copy(src, dst, load_sem.at[i])
        for i, (src, dst) in enumerate(((clu_hbm, clu_ref), (own_hbm, own_ref), (emb_hbm, emb_ref)))
    ]
    for load in loads:
        load.start()
    barrier = pltpu.get_barrier_semaphore()

    @pl.when(is_owner)
    def _():
        def greet(t, c):
            to = OWNERS - 1 - t
            for q in range(SPLITS):
                @pl.when(jnp.logical_not((to == me) & (q == split)))
                def _():
                    pl.semaphore_signal(barrier, inc=1, device_id=(to, q), device_id_type=MESH)
            return c
        lax.fori_loop(0, OWNERS, greet, 0, unroll=UNROLL)

    loads[0].wait()
    loads[1].wait()
    cluster = clu_ref[...]
    hot = (iota((CLUSTERS, ROWS), 0) == cluster).astype(jnp.bfloat16)
    table = (iota((OWNERS, CLUSTERS), 0) == own_ref[...]).astype(jnp.bfloat16)
    owner_hot = jnp.dot(table, hot, preferred_element_type=jnp.float32)
    before = (iota((ROWS, ROWS), 0) < iota((ROWS, ROWS), 1)).astype(jnp.bfloat16)
    count = jnp.dot(owner_hot.astype(jnp.bfloat16), before, preferred_element_type=jnp.float32)
    slot = jnp.sum(
        owner_hot * (count + CAP * iota((OWNERS, ROWS), 0).astype(jnp.float32)), 0, keepdims=True
    ).astype(jnp.int32)
    lane_hot = iota((ROWS, ROWS), 0) == lax.rem(here, 16) * CAP + (slot & (CAP - 1))
    labels = (owner_hot * (cluster + 1).astype(jnp.float32)).astype(jnp.bfloat16)
    lab_send[...] = lax.dot_general(
        labels, lane_hot.astype(jnp.bfloat16), (((1,), (1,)), ((), ())),
        preferred_element_type=jnp.float32,
    )
    loads[2].wait()
    values = emb_ref[...].astype(jnp.float32)
    unit = (values * lax.rsqrt(jnp.sum(values * values, 1, keepdims=True) + 1e-06)).astype(jnp.bfloat16)
    pick = (iota((OWNERS * CAP, ROWS), 0) == slot).astype(jnp.bfloat16)
    parts = [
        jnp.dot(pick, unit[:, h * HALF:(h + 1) * HALF], preferred_element_type=jnp.float32).reshape(
            OWNERS, CAP, HALF
        )
        for h in range(2)
    ]
    send[...] = jnp.concatenate(parts, 1).astype(jnp.bfloat16)
    pl.semaphore_wait(barrier, jnp.where(is_owner, OWNERS - 1, OWNERS))
    first = lax.rem(SPIN_X * split + SPIN_M * me, OWNERS)

    def post(t, c):
        o = lax.rem(first + MULT * t, OWNERS)

        @pl.when(jnp.logical_not(is_owner & (o == mine)))
        def _():
            there = home_of(o)
            pltpu.make_async_remote_copy(
                src_ref=lab_send.at[pl.ds(o, 1)], dst_ref=lab_recv.at[pl.ds(here, 1)],
                send_sem=lab_send_sem, recv_sem=lab_sem, device_id=there, device_id_type=MESH,
            ).start()
            pltpu.make_async_remote_copy(
                src_ref=send.at[o], dst_ref=recv.at[here],
                send_sem=send_sem, recv_sem=recv_sem.at[lax.div(z, 2)], device_id=there, device_id_type=MESH,
            ).start()
        return c
    lax.fori_loop(0, OWNERS, post, 0, unroll=UNROLL)

    @pl.when(is_owner)
    def _():
        recv[here] = send[mine]
        lab_recv[pl.ds(here, 1)] = lab_send[pl.ds(mine, 1)]
        wait_bytes(lab_recv.at[pl.ds(0, DEVICES - 1)], lab_sem)
        labels = jnp.sum(lab_recv[...].reshape(8, 16, 128), 1)
        eye = iota((ROWS, ROWS), 0) == iota((ROWS, ROWS), 1)
        columns = lax.dot_general(
            eye.astype(jnp.bfloat16), labels.astype(jnp.bfloat16), (((1,), (1,)), ((), ())),
            preferred_element_type=jnp.float32,
        )
        tops, wides = [None] * 8, [None] * 8

        def take(begin, end):
            got = recv[begin // CAP:end // CAP].astype(jnp.float32)
            for h in range(2):
                held[begin:end, h * HALF:(h + 1) * HALF] = (
                    got[:, h * CAP:(h + 1) * CAP].reshape(end - begin, HALF).astype(jnp.bfloat16)
                )

        def score(rows, cols):
            scores = lax.dot_general(
                held[rows[0] * 128:rows[1] * 128, :], held[cols[0] * 128:cols[1] * 128, :],
                (((1,), (1,)), ((), ())), preferred_element_type=jnp.float32,
            )
            for i in range(*rows):
                for j in range(*cols):
                    same = columns[:, i:i + 1] == labels[j:j + 1, :]
                    if i == j:
                        same = same & jnp.logical_not(eye)
                    u, v = (i - rows[0]) * 128, (j - cols[0]) * 128
                    kept = jnp.where(same, scores[u:u + 128, v:v + 128], -2.0)
                    top = jnp.max(kept, 0, keepdims=True)
                    tops[j] = top if tops[j] is None else jnp.maximum(tops[j], top)
                    if not cols[0] <= i < cols[1]:
                        wides[i] = kept if wides[i] is None else jnp.maximum(wides[i], kept)

        def close(i):
            if wides[i] is not None:
                tops[i] = jnp.maximum(tops[i], jnp.max(jnp.transpose(wides[i]), 0, keepdims=True))

        def give(src, m, x):
            @pl.when(jnp.logical_not((m == me) & (x == split)))
            def _():
                pltpu.make_async_remote_copy(
                    src_ref=src, dst_ref=ret_recv.at[pl.ds(mine, 1)],
                    send_sem=ret_send_sem, recv_sem=ret_sem, device_id=(m, x), device_id_type=MESH,
                ).start()

        wait_bytes(recv.at[pl.ds(0, DEVICES // 2 - 1)], recv_sem.at[0])
        take(0, 512)
        score((0, 2), (0, 2))
        score((0, 4), (2, 4))
        close(0)
        close(1)
        wait_bytes(recv.at[pl.ds(0, DEVICES // 2)], recv_sem.at[1])
        take(512, 1024)
        score((4, 8), (0, 2))
        for b in range(2):
            soon[b:b + 1, :] = tops[b]
        for m in (1, 0, 9, 8, 3, 2, 11, 10):
            for x in range(SPLITS):
                give(soon.at[pl.ds(x // 2, 1)], m, x)
        score((4, 8), (2, 4))
        score((4, 6), (4, 6))
        score((4, 8), (6, 8))
        for b in range(4, 6):
            close(b)
        for b in range(6, 8):
            close(b)
        for b in range(8):
            best[b:b + 1, :] = tops[b]

        def give_row(m, c):
            z_to, y_to = lax.div(m, 8), lax.rem(lax.div(m, 2), 4)
            block = lax.div(z_to, 2) * 4 + lax.div(y_to, 2) * 2

            @pl.when(block != 0)
            def _():
                for x in range(SPLITS):
                    give(best.at[pl.ds(block + x // 2, 1)], m, x)
            return c
        lax.fori_loop(0, OWNERS, give_row, 0)
        ret_recv[pl.ds(mine, 1)] = best[pl.ds(lax.div(here, 16), 1)]
        wait_bytes(ret_recv.at[pl.ds(0, OWNERS - 1)], ret_sem)

    @pl.when(jnp.logical_not(is_owner))
    def _():
        wait_bytes(ret_recv, ret_sem)
    rest = ret_recv[...]
    terms = []
    for _ in range(3):
        terms.append(rest.astype(jnp.bfloat16))
        rest = rest - terms[-1].astype(jnp.float32)
    spread = lax.dot_general(
        jnp.concatenate(terms, 0), jnp.concatenate([owner_hot.astype(jnp.bfloat16)] * 3, 0),
        (((0,), (0,)), ((), ())), preferred_element_type=jnp.float32,
    )
    out_ref[...] = jnp.sum(jnp.where(lane_hot, spread, 0.0), 0, keepdims=True)
    @pl.when(is_owner)
    def _():
        wait_bytes(send.at[pl.ds(0, OWNERS - 1)], send_sem)
        wait_bytes(lab_send.at[pl.ds(0, OWNERS - 1)], lab_send_sem)
        wait_bytes(lab_recv.at[pl.ds(0, DEVICES - 1)], ret_send_sem)

    @pl.when(jnp.logical_not(is_owner))
    def _():
        wait_bytes(send, send_sem)
        wait_bytes(lab_send, lab_send_sem)


def on_device(emb, cluster, owner_of):
    best = pl.pallas_call(
        kernel,
        out_shape=jax.ShapeDtypeStruct((1, ROWS), jnp.float32),
        in_specs=[pl.BlockSpec(memory_space=pltpu.HBM)] * 3,
        out_specs=pl.BlockSpec(memory_space=pltpu.VMEM),
        scratch_shapes=[
            pltpu.VMEM((ROWS, WIDTH), jnp.bfloat16),
            pltpu.VMEM((1, ROWS), jnp.int32),
            pltpu.VMEM((1, CLUSTERS), jnp.int32),
            pltpu.VMEM((OWNERS, 2 * CAP, HALF), jnp.bfloat16),
            pltpu.VMEM((OWNERS, 128), jnp.float32),
            pltpu.VMEM((DEVICES, 2 * CAP, HALF), jnp.bfloat16),
            pltpu.VMEM((DEVICES, 128), jnp.float32),
            pltpu.VMEM((DEVICES * CAP, WIDTH), jnp.bfloat16),
            pltpu.VMEM((2, 128), jnp.float32),
            pltpu.VMEM((8, 128), jnp.float32),
            pltpu.VMEM((OWNERS, 128), jnp.float32),
            pltpu.SemaphoreType.DMA((3,)),
            pltpu.SemaphoreType.DMA,
            pltpu.SemaphoreType.DMA,
            pltpu.SemaphoreType.DMA,
            pltpu.SemaphoreType.DMA((2,)),
            pltpu.SemaphoreType.DMA,
            pltpu.SemaphoreType.DMA,
        ],
        compiler_params=pltpu.CompilerParams(
            collective_id=0, has_side_effects=True, vmem_limit_bytes=24 * 1024 * 1024
        ),
    )(*[
        pltpu.with_memory_space_constraint(a, pltpu.HBM)
        for a in (emb, cluster.reshape(1, ROWS), owner_of.reshape(1, CLUSTERS))
    ])
    return best.reshape(ROWS)


def solution(mesh):
    return jax.shard_map(
        on_device,
        mesh=mesh,
        in_specs=(P(("owner", "split"), None), P(("owner", "split")), P()),
        out_specs=P(("owner", "split")),
        check_vma=False,
    )
```

time: 28.2 us -> 27.4 us (0.972)
  Pallas kernels: 27.5 us -> 26.7 us
    pallas_call x1, Pallas kernels: 27.5 us -> 26.7 us  [on_device(): pl.pallas_call(kernel, out_shape=jax.ShapeDtypeStruct((1, ROWS), jnp.floa...]
where the time goes in v4:
time: 27.4 us; the launch traced here: 27.3 us
  Pallas kernels  26.7 us (97%)
  local copies, waits for them, and re-layouts  0.51 us (2%)
    pallas_call x1, Pallas kernels, on_device(): pl.pallas_call(kernel, out_shape=jax.ShapeDtypeStruct((1, ROWS), jnp.floa...  26.7 us

profile of v4, /device:TPU:1, one launch (start us, length us, event | category | flops | bytes accessed | tf_op | source)
XLA Modules:
  0.0 27.3 jit_solution(13460827336675775983)
XLA Ops:
  0.0 26.7 %shard_map.37 = f32[1,128]{1,0:T(1,128)S(1)} custom-call(bf16[128,1024]{1,0:T(8,128)(2,1)} %emb_hbm.1, s32[1,128]{1,0:T(1,128)} %bitcast.4, s32[1,64]{1,0:T(1,128)} %bitcast.5), custom_call_target="tpu_custom_call" | custom-call | tf_op jit(solution)/shard_map/pallas_call | solution.py:231
  26.8 0.5 %copy.5 = f32[128]{0:T(128)} copy(f32[128]{0:T(128)S(1)} %bitcast.3) | data formatting | bytes 1024

commit v5 on v4

--- a/solution.py
+++ b/solution.py
@@ -13,6 +13,11 @@
 HALF = WIDTH // 2
 ROWS = 128
 CLUSTERS = 64
+NEARS = ((0, 0), (1, 0), (0, 1), (3, 0), (0, 3), (1, 1), (2, 0), (0, 2))
+NEARS3 = ()
+FAR_CORE = 0
+FAR_DX = (2, 1, 3, 0)
+FAR_DY = (2, 1, 3, 0)
 DEVICES = OWNERS * SPLITS
 GROUPS = 4
 PER = DEVICES // GROUPS
@@ -35,18 +40,66 @@
     pltpu.make_async_copy(ref, ref, sem).wait()
 
 
+def is_near(x, y, z, core):
+    near = z < 0
+    for plane, columns in ((2, NEARS), (3, NEARS3)):
+        for a, b in columns:
+            near = near | ((x == a) & (y == b) & ((z == plane) | (z == 3 - plane)))
+    return near & (core == FAR_CORE)
+
+
+def spot_of(z, y, core, x):
+    return (
+        lax.div(z, 2) * 64 + lax.div(y, 2) * 32 + lax.div(x, 2) * 16
+        + lax.rem(y, 2) * 8 + lax.rem(x, 2) * 4 + lax.rem(z, 2) * 2 + core
+    )
+
+
+def find_slots(cluster, owners, lane):
+    hot = (iota((CLUSTERS, ROWS), 0) == cluster).astype(jnp.bfloat16)
+    table = (iota((OWNERS, CLUSTERS), 0) == owners).astype(jnp.bfloat16)
+    owner_hot = jnp.dot(table, hot, preferred_element_type=jnp.float32)
+    before = (iota((ROWS, ROWS), 0) < iota((ROWS, ROWS), 1)).astype(jnp.bfloat16)
+    count = jnp.dot(owner_hot.astype(jnp.bfloat16), before, preferred_element_type=jnp.float32)
+    slot = jnp.sum(
+        owner_hot * (count + CAP * iota((OWNERS, ROWS), 0).astype(jnp.float32)), 0, keepdims=True
+    ).astype(jnp.int32)
+    lane_hot = iota((ROWS, ROWS), 0) == lane + (slot & (CAP - 1))
+    return owner_hot, slot, lane_hot
+
+
+def fill(values, cluster, owner_hot, slot, lane_hot, send, lab_send):
+    labels = (owner_hot * (cluster + 1).astype(jnp.float32)).astype(jnp.bfloat16)
+    lab_send[...] = lax.dot_general(
+        labels, lane_hot.astype(jnp.bfloat16), (((1,), (1,)), ((), ())),
+        preferred_element_type=jnp.float32,
+    )
+    values = values.astype(jnp.float32)
+    unit = (values * lax.rsqrt(jnp.sum(values * values, 1, keepdims=True) + 1e-06)).astype(jnp.bfloat16)
+    pick = (iota((OWNERS * CAP, ROWS), 0) == slot).astype(jnp.bfloat16)
+    parts = [
+        jnp.dot(pick, unit[:, h * HALF:(h + 1) * HALF], preferred_element_type=jnp.float32).reshape(
+            OWNERS, CAP, HALF
+        )
+        for h in range(2)
+    ]
+    send[...] = jnp.concatenate(parts, 1).astype(jnp.bfloat16)
+
+
 def kernel(
     emb_hbm, clu_hbm, own_hbm, out_ref,
-    emb_ref, clu_ref, own_ref, send, lab_send, recv, lab_recv, held, soon, best, ret_recv,
+    emb_ref, clu_ref, own_ref, send, lab_send, emb_far, clu_far, send_far, lab_far, recv, lab_recv, held, soon, best, ret_recv,
     load_sem, send_sem, lab_send_sem, ret_send_sem, recv_sem, lab_sem, ret_sem,
+    far_send_sem, lab_far_sem, give_sem, got_sem,
 ):
     me = lax.axis_index("owner")
     split = lax.axis_index("split")
     z, y, core = lax.div(me, 8), lax.rem(lax.div(me, 2), 4), lax.rem(me, 2)
-    here = (
-        lax.div(z, 2) * 64 + lax.div(y, 2) * 32 + lax.div(split, 2) * 16
-        + lax.rem(y, 2) * 8 + lax.rem(split, 2) * 4 + lax.rem(z, 2) * 2 + core
-    )
+    here = spot_of(z, y, core, split)
+    near = is_near(split, y, z, core)
+    is_relay = (z < 2) & near
+    is_far = (z >= 2) & near
+    peer = ((3 - z) * 8 + y * 2 + core, split)
     is_owner = (lax.rem(me, 2) == 1) & (me < 16)
     mine = lax.rem(lax.div(me, 2), 8) * 4 + split
     loads = [
@@ -57,64 +110,89 @@
         load.start()
     barrier = pltpu.get_barrier_semaphore()
 
+    @pl.when(is_relay)
+    def _():
+        pl.semaphore_signal(barrier, inc=1, device_id=peer, device_id_type=MESH)
+
     @pl.when(is_owner)
     def _():
         def greet(t, c):
             to = OWNERS - 1 - t
             for q in range(SPLITS):
-                @pl.when(jnp.logical_not((to == me) & (q == split)))
+                ahead = (to >= 16) & is_near(q, lax.rem(lax.div(to, 2), 4), lax.div(to, 8), lax.rem(to, 2))
+
+                @pl.when(jnp.logical_not(ahead | ((to == me) & (q == split))))
                 def _():
                     pl.semaphore_signal(barrier, inc=1, device_id=(to, q), device_id_type=MESH)
             return c
         lax.fori_loop(0, OWNERS, greet, 0, unroll=UNROLL)
 
+    far_copies = [
+        pltpu.make_async_remote_copy(
+            src_ref=src, dst_ref=dst, send_sem=give_sem.at[i], recv_sem=got_sem.at[i],
+            device_id=peer, device_id_type=MESH,
+        )
+        for i, (src, dst) in enumerate(((clu_hbm, clu_far), (emb_hbm, emb_far)))
+    ]
+
+    @pl.when(is_far)
+    def _():
+        pl.semaphore_wait(barrier, 1)
+        for copy in far_copies:
+            copy.start()
+
     loads[0].wait()
     loads[1].wait()
     cluster = clu_ref[...]
-    hot = (iota((CLUSTERS, ROWS), 0) == cluster).astype(jnp.bfloat16)
-    table = (iota((OWNERS, CLUSTERS), 0) == own_ref[...]).astype(jnp.bfloat16)
-    owner_hot = jnp.dot(table, hot, preferred_element_type=jnp.float32)
-    before = (iota((ROWS, ROWS), 0) < iota((ROWS, ROWS), 1)).astype(jnp.bfloat16)
-    count = jnp.dot(owner_hot.astype(jnp.bfloat16), before, preferred_element_type=jnp.float32)
-    slot = jnp.sum(
-        owner_hot * (count + CAP * iota((OWNERS, ROWS), 0).astype(jnp.float32)), 0, keepdims=True
-    ).astype(jnp.int32)
-    lane_hot = iota((ROWS, ROWS), 0) == lax.rem(here, 16) * CAP + (slot & (CAP - 1))
-    labels = (owner_hot * (cluster + 1).astype(jnp.float32)).astype(jnp.bfloat16)
-    lab_send[...] = lax.dot_general(
-        labels, lane_hot.astype(jnp.bfloat16), (((1,), (1,)), ((), ())),
-        preferred_element_type=jnp.float32,
-    )
+    owner_hot, slot, lane_hot = find_slots(cluster, own_ref[...], lax.rem(here, 16) * CAP)
     loads[2].wait()
-    values = emb_ref[...].astype(jnp.float32)
-    unit = (values * lax.rsqrt(jnp.sum(values * values, 1, keepdims=True) + 1e-06)).astype(jnp.bfloat16)
-    pick = (iota((OWNERS * CAP, ROWS), 0) == slot).astype(jnp.bfloat16)
-    parts = [
-        jnp.dot(pick, unit[:, h * HALF:(h + 1) * HALF], preferred_element_type=jnp.float32).reshape(
-            OWNERS, CAP, HALF
+
+    @pl.when(jnp.logical_not(is_far))
+    def _():
+        fill(emb_ref[...], cluster, owner_hot, slot, lane_hot, send, lab_send)
+
+    @pl.when(jnp.logical_not(is_far))
+    def _():
+        pl.semaphore_wait(barrier, jnp.where(is_owner, OWNERS - 1, OWNERS))
+
+    first = lax.rem(SPIN_X * split + SPIN_M * me, OWNERS)
+
+    def send_step(o, spot, rows, labels, rows_sem, labels_sem):
+        there = home_of(o)
+        pltpu.make_async_remote_copy(
+            src_ref=labels.at[pl.ds(o, 1)], dst_ref=lab_recv.at[pl.ds(spot, 1)],
+            send_sem=labels_sem, recv_sem=lab_sem, device_id=there, device_id_type=MESH,
+        ).start()
+        pltpu.make_async_remote_copy(
+            src_ref=rows.at[o], dst_ref=recv.at[spot],
+            send_sem=rows_sem, recv_sem=recv_sem.at[lax.div(spot, 64)], device_id=there, device_id_type=MESH,
+        ).start()
+
+    @pl.when(jnp.logical_not(is_far))
+    def _():
+        def post(t, c):
+            o = lax.rem(first + MULT * t, OWNERS)
+
+            @pl.when(jnp.logical_not(is_owner & (o == mine)))
+            def _():
+                send_step(o, here, send, lab_send, send_sem, lab_send_sem)
+            return c
+        lax.fori_loop(0, OWNERS, post, 0, unroll=UNROLL)
+
+    @pl.when(is_relay)
+    def _():
+        for copy in far_copies:
+            copy.wait_recv()
+        cluster = clu_far[...]
+        spot = spot_of(3 - z, y, core, split)
+        fill(
+            emb_far[...], cluster, *find_slots(cluster, own_ref[...], lax.rem(spot, 16) * CAP), send_far, lab_far
         )
-        for h in range(2)
-    ]
-    send[...] = jnp.concatenate(parts, 1).astype(jnp.bfloat16)
-    pl.semaphore_wait(barrier, jnp.where(is_owner, OWNERS - 1, OWNERS))
-    first = lax.rem(SPIN_X * split + SPIN_M * me, OWNERS)
-
-    def post(t, c):
-        o = lax.rem(first + MULT * t, OWNERS)
-
-        @pl.when(jnp.logical_not(is_owner & (o == mine)))
-        def _():
-            there = home_of(o)
-            pltpu.make_async_remote_copy(
-                src_ref=lab_send.at[pl.ds(o, 1)], dst_ref=lab_recv.at[pl.ds(here, 1)],
-                send_sem=lab_send_sem, recv_sem=lab_sem, device_id=there, device_id_type=MESH,
-            ).start()
-            pltpu.make_async_remote_copy(
-                src_ref=send.at[o], dst_ref=recv.at[here],
-                send_sem=send_sem, recv_sem=recv_sem.at[lax.div(z, 2)], device_id=there, device_id_type=MESH,
-            ).start()
-        return c
-    lax.fori_loop(0, OWNERS, post, 0, unroll=UNROLL)
+        for dx in FAR_DX:
+            for dy in FAR_DY:
+                for plane in range(2):
+                    o = plane * 16 + lax.rem(y + dy, 4) * 4 + lax.rem(split + dx, 4)
+                    send_step(o, spot, send_far, lab_far, far_send_sem, lab_far_sem)
 
     @pl.when(is_owner)
     def _():
@@ -221,10 +299,20 @@
         wait_bytes(lab_send.at[pl.ds(0, OWNERS - 1)], lab_send_sem)
         wait_bytes(lab_recv.at[pl.ds(0, DEVICES - 1)], ret_send_sem)
 
-    @pl.when(jnp.logical_not(is_owner))
+    @pl.when(jnp.logical_not(is_owner | is_far))
     def _():
         wait_bytes(send, send_sem)
         wait_bytes(lab_send, lab_send_sem)
+
+    @pl.when(is_far)
+    def _():
+        for copy in far_copies:
+            copy.wait_send()
+
+    @pl.when(is_relay)
+    def _():
+        wait_bytes(send_far, far_send_sem)
+        wait_bytes(lab_far, lab_far_sem)
 
 
 def on_device(emb, cluster, owner_of):
@@ -239,6 +327,10 @@
             pltpu.VMEM((1, CLUSTERS), jnp.int32),
             pltpu.VMEM((OWNERS, 2 * CAP, HALF), jnp.bfloat16),
             pltpu.VMEM((OWNERS, 128), jnp.float32),
+            pltpu.VMEM((ROWS, WIDTH), jnp.bfloat16),
+            pltpu.VMEM((1, ROWS), jnp.int32),
+            pltpu.VMEM((OWNERS, 2 * CAP, HALF), jnp.bfloat16),
+            pltpu.VMEM((OWNERS, 128), jnp.float32),
             pltpu.VMEM((DEVICES, 2 * CAP, HALF), jnp.bfloat16),
             pltpu.VMEM((DEVICES, 128), jnp.float32),
             pltpu.VMEM((DEVICES * CAP, WIDTH), jnp.bfloat16),
@@ -252,6 +344,10 @@
             pltpu.SemaphoreType.DMA((2,)),
             pltpu.SemaphoreType.DMA,
             pltpu.SemaphoreType.DMA,
+            pltpu.SemaphoreType.DMA,
+            pltpu.SemaphoreType.DMA,
+            pltpu.SemaphoreType.DMA((2,)),
+            pltpu.SemaphoreType.DMA((2,)),
         ],
         compiler_params=pltpu.CompilerParams(
             collective_id=0, has_side_effects=True, vmem_limit_bytes=24 * 1024 * 1024

time: 27.4 us -> 26.2 us (0.956)
  Pallas kernels: 26.7 us -> 25.6 us
    pallas_call x1, Pallas kernels: 26.7 us -> 25.6 us  [on_device(): pl.pallas_call(kernel, out_shape=jax.ShapeDtypeStruct((1, ROWS), jnp.floa...]
where the time goes in v5:
time: 26.2 us; the launch traced here: 26.1 us
  Pallas kernels  25.6 us (98%)
  local copies, waits for them, and re-layouts  0.51 us (2%)
    pallas_call x1, Pallas kernels, on_device(): pl.pallas_call(kernel, out_shape=jax.ShapeDtypeStruct((1, ROWS), jnp.floa...  25.6 us

profile of v5, /device:TPU:1, one launch (start us, length us, event | category | flops | bytes accessed | tf_op | source)
XLA Modules:
  0.0 26.1 jit_solution(15375751310048054957)
XLA Ops:
  0.0 25.6 %shard_map.37 = f32[1,128]{1,0:T(1,128)S(1)} custom-call(bf16[128,1024]{1,0:T(8,128)(2,1)} %emb_hbm.1, s32[1,128]{1,0:T(1,128)} %bitcast.4, s32[1,64]{1,0:T(1,128)} %bitcast.5), custom_call_target="tpu_custom_call" | custom-call | tf_op jit(solution)/shard_map/pallas_call | solution.py:319
  25.6 0.5 %copy.5 = f32[128]{0:T(128)} copy(f32[128]{0:T(128)S(1)} %bitcast.3) | data formatting | bytes 1024

commit v6 on v5

--- a/solution.py
+++ b/solution.py
@@ -13,9 +13,6 @@
 HALF = WIDTH // 2
 ROWS = 128
 CLUSTERS = 64
-NEARS = ((0, 0), (1, 0), (0, 1), (3, 0), (0, 3), (1, 1), (2, 0), (0, 2))
-NEARS3 = ()
-FAR_CORE = 0
 FAR_DX = (2, 1, 3, 0)
 FAR_DY = (2, 1, 3, 0)
 DEVICES = OWNERS * SPLITS
@@ -23,7 +20,7 @@
 PER = DEVICES // GROUPS
 GROUP_ROWS = PER * CAP
 UNROLL = 4
-MULT = 1
+PN = 12
 SPIN_X = 4
 SPIN_M = 8
 
@@ -38,14 +35,6 @@
 
 def wait_bytes(ref, sem):
     pltpu.make_async_copy(ref, ref, sem).wait()
-
-
-def is_near(x, y, z, core):
-    near = z < 0
-    for plane, columns in ((2, NEARS), (3, NEARS3)):
-        for a, b in columns:
-            near = near | ((x == a) & (y == b) & ((z == plane) | (z == 3 - plane)))
-    return near & (core == FAR_CORE)
 
 
 def spot_of(z, y, core, x):
@@ -96,9 +85,9 @@
     split = lax.axis_index("split")
     z, y, core = lax.div(me, 8), lax.rem(lax.div(me, 2), 4), lax.rem(me, 2)
     here = spot_of(z, y, core, split)
-    near = is_near(split, y, z, core)
-    is_relay = (z < 2) & near
-    is_far = (z >= 2) & near
+    is_far = (z == 2) & (core == 0)
+    is_relay = (z == 1) & (core == 0)
+    is_paced = (z >= 2) & (core == 1)
     peer = ((3 - z) * 8 + y * 2 + core, split)
     is_owner = (lax.rem(me, 2) == 1) & (me < 16)
     mine = lax.rem(lax.div(me, 2), 8) * 4 + split
@@ -119,7 +108,7 @@
         def greet(t, c):
             to = OWNERS - 1 - t
             for q in range(SPLITS):
-                ahead = (to >= 16) & is_near(q, lax.rem(lax.div(to, 2), 4), lax.div(to, 8), lax.rem(to, 2))
+                ahead = (lax.div(to, 8) == 2) & (lax.rem(to, 2) == 0)
 
                 @pl.when(jnp.logical_not(ahead | ((to == me) & (q == split))))
                 def _():
@@ -171,13 +160,18 @@
     @pl.when(jnp.logical_not(is_far))
     def _():
         def post(t, c):
-            o = lax.rem(first + MULT * t, OWNERS)
+            o = jnp.where(z >= 2, lax.div(t, 16) * 16 + lax.rem(first + t, 16), lax.rem(first + t, OWNERS))
 
             @pl.when(jnp.logical_not(is_owner & (o == mine)))
             def _():
                 send_step(o, here, send, lab_send, send_sem, lab_send_sem)
             return c
-        lax.fori_loop(0, OWNERS, post, 0, unroll=UNROLL)
+        lax.fori_loop(0, PN, post, 0, unroll=UNROLL)
+
+        @pl.when(is_paced)
+        def _():
+            wait_bytes(send.at[pl.ds(0, PN)], send_sem)
+        lax.fori_loop(PN, OWNERS, post, 0, unroll=UNROLL)
 
     @pl.when(is_relay)
     def _():
@@ -301,7 +295,13 @@
 
     @pl.when(jnp.logical_not(is_owner | is_far))
     def _():
-        wait_bytes(send, send_sem)
+        @pl.when(is_paced)
+        def _():
+            wait_bytes(send.at[pl.ds(0, OWNERS - PN)], send_sem)
+
+        @pl.when(jnp.logical_not(is_paced))
+        def _():
+            wait_bytes(send, send_sem)
         wait_bytes(lab_send, lab_send_sem)
 
     @pl.when(is_far)

time: 26.2 us -> 26 us (level)
  Pallas kernels: 25.6 us -> 25.3 us
where the time goes in v6:
time: 26 us; the launch traced here: 25.8 us
  Pallas kernels  25.3 us (97%)
  local copies, waits for them, and re-layouts  0.51 us (2%)
    pallas_call x1, Pallas kernels, on_device(): pl.pallas_call(kernel, out_shape=jax.ShapeDtypeStruct((1, ROWS), jnp.floa...  25.3 us

profile of v6, /device:TPU:1, one launch (start us, length us, event | category | flops | bytes accessed | tf_op | source)
XLA Modules:
  0.0 25.8 jit_solution(18248739212569023882)
XLA Ops:
  0.0 25.3 %shard_map.37 = f32[1,128]{1,0:T(1,128)S(1)} custom-call(bf16[128,1024]{1,0:T(8,128)(2,1)} %emb_hbm.1, s32[1,128]{1,0:T(1,128)} %bitcast.4, s32[1,64]{1,0:T(1,128)} %bitcast.5), custom_call_target="tpu_custom_call" | custom-call | tf_op jit(solution)/shard_map/pallas_call | solution.py:319
  25.3 0.5 %copy.5 = f32[128]{0:T(128)} copy(f32[128]{0:T(128)S(1)} %bitcast.3) | data formatting | bytes 1024

commit v7 on v6

--- a/solution.py
+++ b/solution.py
@@ -20,7 +20,7 @@
 PER = DEVICES // GROUPS
 GROUP_ROWS = PER * CAP
 UNROLL = 4
-PN = 12
+PN = 16
 SPIN_X = 4
 SPIN_M = 8
 
@@ -239,12 +239,12 @@
 
         wait_bytes(recv.at[pl.ds(0, DEVICES // 2 - 1)], recv_sem.at[0])
         take(0, 512)
+        wait_bytes(recv.at[pl.ds(0, DEVICES // 2)], recv_sem.at[1])
+        take(512, 1024)
         score((0, 2), (0, 2))
         score((0, 4), (2, 4))
         close(0)
         close(1)
-        wait_bytes(recv.at[pl.ds(0, DEVICES // 2)], recv_sem.at[1])
-        take(512, 1024)
         score((4, 8), (0, 2))
         for b in range(2):
             soon[b:b + 1, :] = tops[b]
@@ -282,11 +282,10 @@
     for _ in range(3):
         terms.append(rest.astype(jnp.bfloat16))
         rest = rest - terms[-1].astype(jnp.float32)
-    spread = lax.dot_general(
-        jnp.concatenate(terms, 0), jnp.concatenate([owner_hot.astype(jnp.bfloat16)] * 3, 0),
-        (((0,), (0,)), ((), ())), preferred_element_type=jnp.float32,
-    )
-    out_ref[...] = jnp.sum(jnp.where(lane_hot, spread, 0.0), 0, keepdims=True)
+    picked = jnp.dot(jnp.concatenate(terms, 0), lane_hot.astype(jnp.bfloat16), preferred_element_type=jnp.float32)
+    picked = picked[0:OWNERS] + (picked[OWNERS:2 * OWNERS] + picked[2 * OWNERS:])
+    out_ref[...] = jnp.sum(picked * owner_hot, 0, keepdims=True)
+
     @pl.when(is_owner)
     def _():
         wait_bytes(send.at[pl.ds(0, OWNERS - 1)], send_sem)

time: 26 us -> 26 us (level)
  no operation moved by 1% of the time
where the time goes in v7:
time: 26 us; the launch traced here: 25.9 us
  Pallas kernels  25.3 us (97%)
  local copies, waits for them, and re-layouts  0.51 us (2%)
    pallas_call x1, Pallas kernels, on_device(): pl.pallas_call(kernel, out_shape=jax.ShapeDtypeStruct((1, ROWS), jnp.floa...  25.3 us

profile of v7, /device:TPU:1, one launch (start us, length us, event | category | flops | bytes accessed | tf_op | source)
XLA Modules:
  0.0 25.9 jit_solution(4990644562678817857)
XLA Ops:
  0.0 25.3 %shard_map.37 = f32[1,128]{1,0:T(1,128)S(1)} custom-call(bf16[128,1024]{1,0:T(8,128)(2,1)} %emb_hbm.1, s32[1,128]{1,0:T(1,128)} %bitcast.4, s32[1,64]{1,0:T(1,128)} %bitcast.5), custom_call_target="tpu_custom_call" | custom-call | tf_op jit(solution)/shard_map/pallas_call | solution.py:318
  25.4 0.5 %copy.5 = f32[128]{0:T(128)} copy(f32[128]{0:T(128)S(1)} %bitcast.3) | data formatting | bytes 1024

commit v8 on v7

--- a/solution.py
+++ b/solution.py
@@ -20,9 +20,9 @@
 PER = DEVICES // GROUPS
 GROUP_ROWS = PER * CAP
 UNROLL = 4
-PN = 16
-SPIN_X = 4
-SPIN_M = 8
+PN = 14
+SPIN_X = 5
+SPIN_M = 2
 
 
 def home_of(o):

time: 26 us -> 25.9 us (level)
  no operation moved by 1% of the time
where the time goes in v8:
time: 25.9 us; the launch traced here: 25.7 us
  Pallas kernels  25.2 us (97%)
  local copies, waits for them, and re-layouts  0.51 us (2%)
    pallas_call x1, Pallas kernels, on_device(): pl.pallas_call(kernel, out_shape=jax.ShapeDtypeStruct((1, ROWS), jnp.floa...  25.2 us

profile of v8, /device:TPU:1, one launch (start us, length us, event | category | flops | bytes accessed | tf_op | source)
XLA Modules:
  0.0 25.7 jit_solution(8957723749435529257)
XLA Ops:
  0.0 25.2 %shard_map.37 = f32[1,128]{1,0:T(1,128)S(1)} custom-call(bf16[128,1024]{1,0:T(8,128)(2,1)} %emb_hbm.1, s32[1,128]{1,0:T(1,128)} %bitcast.4, s32[1,64]{1,0:T(1,128)} %bitcast.5), custom_call_target="tpu_custom_call" | custom-call | tf_op jit(solution)/shard_map/pallas_call | solution.py:318
  25.2 0.5 %copy.5 = f32[128]{0:T(128)} copy(f32[128]{0:T(128)S(1)} %bitcast.3) | data formatting | bytes 1024

commit v9 on v8

--- a/solution.py
+++ b/solution.py
@@ -20,7 +20,7 @@
 PER = DEVICES // GROUPS
 GROUP_ROWS = PER * CAP
 UNROLL = 4
-PN = 14
+PACES = ((12, 3), (16, 2))
 SPIN_X = 5
 SPIN_M = 2
 
@@ -166,12 +166,15 @@
             def _():
                 send_step(o, here, send, lab_send, send_sem, lab_send_sem)
             return c
-        lax.fori_loop(0, PN, post, 0, unroll=UNROLL)
-
-        @pl.when(is_paced)
-        def _():
-            wait_bytes(send.at[pl.ds(0, PN)], send_sem)
-        lax.fori_loop(PN, OWNERS, post, 0, unroll=UNROLL)
+        begin = 0
+        for count, plane in PACES:
+            lax.fori_loop(begin, count, post, 0, unroll=UNROLL)
+            begin = count
+
+            @pl.when(is_paced & (z == plane))
+            def _():
+                wait_bytes(send.at[pl.ds(0, count)], send_sem)
+        lax.fori_loop(begin, OWNERS, post, 0, unroll=UNROLL)
 
     @pl.when(is_relay)
     def _():
@@ -294,9 +297,10 @@
 
     @pl.when(jnp.logical_not(is_owner | is_far))
     def _():
-        @pl.when(is_paced)
-        def _():
-            wait_bytes(send.at[pl.ds(0, OWNERS - PN)], send_sem)
+        for count, plane in PACES:
+            @pl.when(is_paced & (z == plane))
+            def _():
+                wait_bytes(send.at[pl.ds(0, OWNERS - count)], send_sem)
 
         @pl.when(jnp.logical_not(is_paced))
         def _():

time: 25.9 us -> 25.8 us (level)
  no operation moved by 1% of the time
where the time goes in v9:
time: 25.8 us; the launch traced here: 25.7 us
  Pallas kernels  25.2 us (98%)
  local copies, waits for them, and re-layouts  0.51 us (2%)
    pallas_call x1, Pallas kernels, on_device(): pl.pallas_call(kernel, out_shape=jax.ShapeDtypeStruct((1, ROWS), jnp.floa...  25.2 us

profile of v9, /device:TPU:1, one launch (start us, length us, event | category | flops | bytes accessed | tf_op | source)
XLA Modules:
  0.0 25.7 jit_solution(108385310496913049)
XLA Ops:
  0.0 25.2 %shard_map.37 = f32[1,128]{1,0:T(1,128)S(1)} custom-call(bf16[128,1024]{1,0:T(8,128)(2,1)} %emb_hbm.1, s32[1,128]{1,0:T(1,128)} %bitcast.4, s32[1,64]{1,0:T(1,128)} %bitcast.5), custom_call_target="tpu_custom_call" | custom-call | tf_op jit(solution)/shard_map/pallas_call | solution.py:322
  25.2 0.5 %copy.5 = f32[128]{0:T(128)} copy(f32[128]{0:T(128)S(1)} %bitcast.3) | data formatting | bytes 1024

commit v10 on v7

--- a/solution.py
+++ b/solution.py
@@ -42,6 +42,10 @@
         lax.div(z, 2) * 64 + lax.div(y, 2) * 32 + lax.div(x, 2) * 16
         + lax.rem(y, 2) * 8 + lax.rem(x, 2) * 4 + lax.rem(z, 2) * 2 + core
     )
+
+
+def far_first(i):
+    return jnp.where(i == 0, 2, jnp.where(i == 1, 1, jnp.where(i == 2, 3, 0)))
 
 
 def find_slots(cluster, owners, lane):
@@ -160,7 +164,11 @@
     @pl.when(jnp.logical_not(is_far))
     def _():
         def post(t, c):
-            o = jnp.where(z >= 2, lax.div(t, 16) * 16 + lax.rem(first + t, 16), lax.rem(first + t, OWNERS))
+            at = jnp.where(z >= 2, lax.rem(t, 16), lax.div(t, 2))
+            to_plane = jnp.where(z >= 2, lax.div(t, 16), lax.rem(t, 2))
+            dx, dy = far_first(lax.div(at, 4)), far_first(lax.rem(at, 4))
+            ordered = to_plane * 16 + lax.rem(y + dy, 4) * 4 + lax.rem(split + dx, 4)
+            o = jnp.where(z >= 2, to_plane * 16 + lax.rem(first + t, 16), ordered)
 
             @pl.when(jnp.logical_not(is_owner & (o == mine)))
             def _():

time: 26 us -> 26 us (level)
  no operation moved by 1% of the time
where the time goes in v10:
time: 26 us; the launch traced here: 25.9 us
  Pallas kernels  25.3 us (97%)
  local copies, waits for them, and re-layouts  0.51 us (2%)
    pallas_call x1, Pallas kernels, on_device(): pl.pallas_call(kernel, out_shape=jax.ShapeDtypeStruct((1, ROWS), jnp.floa...  25.3 us

profile of v10, /device:TPU:1, one launch (start us, length us, event | category | flops | bytes accessed | tf_op | source)
XLA Modules:
  0.0 25.9 jit_solution(8818591184377220644)
XLA Ops:
  0.0 25.3 %shard_map.37 = f32[1,128]{1,0:T(1,128)S(1)} custom-call(bf16[128,1024]{1,0:T(8,128)(2,1)} %emb_hbm.1, s32[1,128]{1,0:T(1,128)} %bitcast.4, s32[1,64]{1,0:T(1,128)} %bitcast.5), custom_call_target="tpu_custom_call" | custom-call | tf_op jit(solution)/shard_map/pallas_call | solution.py:326
  25.4 0.5 %copy.5 = f32[128]{0:T(128)} copy(f32[128]{0:T(128)S(1)} %bitcast.3) | data formatting | bytes 1024
